TPU v7x, 128 devices: a whole 4x4x4 slice. The times are simulated.
128 devices in a mesh: ctx: 4 (over z_lo, core), resp: 32 (over z_hi, y, x).
Axes of the slice: x: 4, y: 4, z: 4 (z_hi: 2, z_lo: 2; z = z_hi * 2 + z_lo), core: 2. Of those that a mesh axis runs over, the one named last changes fastest.
Arguments:
- prompt_q: bfloat16 [32, 768, 4096], P('resp', 'ctx'), may hold values from -6 to 6
- prompt_kv: bfloat16 [32, 768, 1024], P('resp', 'ctx'), may hold values from -6 to 6
- prompt_cot: bfloat16 [32, 768, 4096], P('resp', 'ctx'), may hold values from -6 to 6
- resp_q: bfloat16 [128, 64, 4096], P('resp'), may hold values from -6 to 6
- resp_kv: bfloat16 [128, 64, 1024], P('resp'), may hold values from -6 to 6
- resp_cot: bfloat16 [128, 64, 4096], P('resp'), may hold values from -6 to 6
- resp_prompt: int32 [128, 1], P('resp'), may hold values from 0 to 31
- tree_end: int32 [128, 64], P('resp'), may hold values from 2 to 64, as said below
- rewards: int32 [128], P('resp'), may hold values from 0 to 10
Outputs:
- d_prompt_q: bfloat16 [32, 768, 4096], P('resp', 'ctx')
- d_prompt_kv: bfloat16 [32, 768, 1024], P('resp', 'ctx')
- d_resp_q: bfloat16 [128, 64, 4096], P('resp')
- d_resp_kv: bfloat16 [128, 64, 1024], P('resp')
Inputs may be any that keep to these rules, and one draw needn't show every extreme that they name: `resp_prompt`: every prompt is the prompt of at least one response. Each response tree's tokens stand in depth-first order with token 0 as its only root: tree_end[i, u] > u, token 0's entry is 64, and the spans of two tokens are nested or apart.
All inputs are finite; a program needn't handle non-finite values.
Results may differ from a plain program's by a relative error of at most 0.029.
Values may be sent and summed in bfloat16 or wider, within the bound.
A program may use at most 192 MiB of HBM per device.

v0:
```python
from functools import reduce
import math

import jax
import jax.numpy as jnp
from jax import lax
from jax.sharding import PartitionSpec as P

HEADS = 32
KV_HEADS = 4
HEAD_DIM = 128


def merged(part, axis, combine):
    gathered = jax.tree.map(lambda a: lax.all_gather(a, axis), part)

    def take(source):
        return jax.tree.map(lambda a: lax.dynamic_index_in_dim(a, source, 0, False), gathered)

    return lax.fori_loop(
        1, lax.axis_size(axis), lambda source, state: combine(state, take(source)), take(0)
    )


def head_scores(queries, key_rows, scaling):
    return (
        jnp.einsum("rlkgd,rmkd->rkglm", queries, key_rows, preferred_element_type=jnp.float32)
        * scaling
    )


def keep_stats(highest, totals):
    return (highest, totals)


def keep_output(output):
    return output


def merge_stats(former, latter):
    highest = jnp.maximum(former[0], latter[0])
    return (
        highest,
        former[1] * jnp.exp(former[0] - highest) + latter[1] * jnp.exp(latter[0] - highest),
    )


def attend(queries, cotangent, pieces, scaling, combine_stats, combine_output):
    scores = [
        jnp.where(entry[2], head_scores(queries, entry[0], scaling), -jnp.inf) for entry in pieces
    ]
    highest = reduce(jnp.maximum, [jnp.max(piece_scores, axis=-1) for piece_scores in scores])
    totals = reduce(
        jnp.add,
        [jnp.sum(jnp.exp(piece_scores - highest[..., None]), axis=-1) for piece_scores in scores],
    )
    highest, totals = combine_stats(highest, totals)
    log_total = highest + jnp.log(totals)
    weights = [jnp.exp(piece_scores - log_total[..., None]) for piece_scores in scores]
    narrowed = [weight.astype(jnp.bfloat16) for weight in weights]
    output = reduce(
        jnp.add,
        [
            jnp.einsum(
                "rkglm,rmkd->rlkgd", narrow_weight, entry[1], preferred_element_type=jnp.float32
            )
            for narrow_weight, entry in zip(narrowed, pieces)
        ],
    )
    output = combine_output(output)
    row_delta = jnp.transpose(
        jnp.sum(cotangent.astype(jnp.float32) * output, axis=-1), (0, 2, 3, 1)
    )
    grad_query = jnp.zeros(queries.shape, jnp.float32)
    key_grads = []
    for weight, narrow_weight, entry in zip(weights, narrowed, pieces):
        grad_prob = jnp.einsum(
            "rlkgd,rmkd->rkglm", cotangent, entry[1], preferred_element_type=jnp.float32
        )
        grad_score = (weight * (grad_prob - row_delta[..., None])).astype(jnp.bfloat16)
        grad_query = (
            grad_query
            + jnp.einsum(
                "rkglm,rmkd->rlkgd", grad_score, entry[0], preferred_element_type=jnp.float32
            )
            * scaling
        )
        grad_keys = (
            jnp.einsum("rkglm,rlkgd->rmkd", grad_score, queries, preferred_element_type=jnp.float32)
            * scaling
        )
        grad_values = jnp.einsum(
            "rkglm,rlkgd->rmkd", narrow_weight, cotangent, preferred_element_type=jnp.float32
        )
        key_grads.append((grad_keys, grad_values))
    return (grad_query, key_grads)


def body(
    prompt_q, prompt_kv, prompt_cot, resp_q, resp_kv, resp_cot, resp_prompt, tree_end, rewards
):
    scaling = 1.0 / math.sqrt(HEAD_DIM)
    group_size = HEADS // KV_HEADS
    kv_width = KV_HEADS * HEAD_DIM
    context_count = lax.axis_size("ctx")
    context_index = lax.axis_index("ctx")
    prompt_count = lax.axis_size("resp")
    prompt_rows = prompt_q.shape[1]
    own_prompt = lax.all_gather(prompt_kv[0], "ctx", axis=0, tiled=True)
    prompt_length = own_prompt.shape[0]
    prompt_queries = prompt_q[0].reshape(1, prompt_rows, KV_HEADS, group_size, HEAD_DIM)
    prompt_grad_out = prompt_cot[0].reshape(1, prompt_rows, KV_HEADS, group_size, HEAD_DIM)
    prompt_keys = own_prompt[:, :kv_width].reshape(1, prompt_length, KV_HEADS, HEAD_DIM)
    prompt_values = own_prompt[:, kv_width:].reshape(1, prompt_length, KV_HEADS, HEAD_DIM)
    query_places = context_index * prompt_rows + jnp.arange(prompt_rows, dtype=jnp.int32)
    key_places = jnp.arange(prompt_length, dtype=jnp.int32)
    causal = (key_places[None, :] <= query_places[:, None])[None, None, None]
    prompt_grad_q, prompt_pieces = attend(
        prompt_queries,
        prompt_grad_out,
        [(prompt_keys, prompt_values, causal)],
        scaling,
        keep_stats,
        keep_output,
    )
    self_terms = jnp.concatenate(
        [
            prompt_pieces[0][0].reshape(prompt_length, kv_width),
            prompt_pieces[0][1].reshape(prompt_length, kv_width),
        ],
        axis=1,
    )
    self_grads = lax.psum_scatter(
        self_terms.astype(jnp.bfloat16), "ctx", scatter_dimension=0, tiled=True
    ).astype(jnp.float32)
    routes = resp_prompt[:, 0]
    onehot = (routes[:, None] == jnp.arange(prompt_count, dtype=jnp.int32)[None, :]).astype(
        jnp.float32
    )
    reward_values = rewards.astype(jnp.float32)
    counts, reward_sums, reward_squares = lax.psum(
        (
            jnp.sum(onehot, axis=0),
            jnp.sum(onehot * reward_values[:, None], axis=0),
            jnp.sum(onehot * (reward_values * reward_values)[:, None], axis=0),
        ),
        "resp",
    )
    means = reward_sums / counts
    spread = jnp.sqrt(reward_squares * counts - reward_sums * reward_sums) / counts
    advantage = (reward_values - jnp.sum(onehot * means[None, :], axis=1)) / jnp.maximum(
        jnp.sum(onehot * spread[None, :], axis=1), 1.0
    )
    responses_here = resp_q.shape[0]
    resp_length = resp_q.shape[1]
    resp_grad_out = (advantage[:, None, None] * resp_cot.astype(jnp.float32)).astype(jnp.bfloat16)
    query_spots = jnp.arange(resp_length, dtype=jnp.int32)
    everywhere = jnp.ones((1, 1, 1, 1, 1), jnp.bool_)
    tiles = lax.all_gather(prompt_kv, "resp", axis=0, tiled=True)
    chosen = tiles[routes]
    block_size = resp_length // context_count
    queries = resp_q.reshape(responses_here, resp_length, KV_HEADS, group_size, HEAD_DIM)
    grad_out = resp_grad_out.reshape(responses_here, resp_length, KV_HEADS, group_size, HEAD_DIM)
    chosen_keys = chosen[:, :, :kv_width].reshape(responses_here, prompt_rows, KV_HEADS, HEAD_DIM)
    chosen_values = chosen[:, :, kv_width:].reshape(responses_here, prompt_rows, KV_HEADS, HEAD_DIM)
    own_rows = lax.dynamic_slice_in_dim(resp_kv, context_index * block_size, block_size, 1)
    tree_keys = own_rows[:, :, :kv_width].reshape(responses_here, block_size, KV_HEADS, HEAD_DIM)
    tree_values = own_rows[:, :, kv_width:].reshape(responses_here, block_size, KV_HEADS, HEAD_DIM)
    tree_ends = lax.dynamic_slice_in_dim(tree_end, context_index * block_size, block_size, 1)
    key_spots = context_index * block_size + jnp.arange(block_size, dtype=jnp.int32)
    tree_mask = (key_spots[None, None, :] <= query_spots[None, :, None]) & (
        query_spots[None, :, None] < tree_ends[:, None, :]
    )

    def merge_scores(highest, totals):
        return merged((highest, totals), "ctx", merge_stats)

    def sum_output(output):
        return lax.psum(output.astype(jnp.bfloat16), "ctx").astype(jnp.float32)

    grad_query, key_grads = attend(
        queries,
        grad_out,
        [
            (chosen_keys, chosen_values, everywhere),
            (tree_keys, tree_values, tree_mask[:, None, None]),
        ],
        scaling,
        merge_scores,
        sum_output,
    )
    tree_terms = jnp.concatenate(
        [
            key_grads[1][0].reshape(responses_here, block_size, kv_width),
            key_grads[1][1].reshape(responses_here, block_size, kv_width),
        ],
        axis=2,
    )
    tree_full = lax.dynamic_update_slice_in_dim(
        jnp.zeros((responses_here, resp_length, 2 * kv_width), jnp.float32),
        tree_terms,
        context_index * block_size,
        1,
    )
    query_sum, tree_sum = (
        lax.psum(
            grad_query.reshape(responses_here, resp_length, HEADS * HEAD_DIM).astype(jnp.bfloat16),
            "ctx",
        ).astype(jnp.float32),
        lax.psum(tree_full.astype(jnp.bfloat16), "ctx").astype(jnp.float32),
    )
    grad_resp_q = query_sum.astype(jnp.bfloat16)
    grad_resp_kv = tree_sum.astype(jnp.bfloat16)
    prompt_terms = jnp.concatenate(
        [
            key_grads[0][0].reshape(responses_here, prompt_rows, kv_width),
            key_grads[0][1].reshape(responses_here, prompt_rows, kv_width),
        ],
        axis=2,
    )
    per_prompt = jnp.einsum("rp,rmx->pmx", onehot, prompt_terms, precision=lax.Precision.HIGHEST)
    returned = lax.psum_scatter(
        per_prompt.astype(jnp.bfloat16), "resp", scatter_dimension=0, tiled=True
    ).astype(jnp.float32)[0]
    grad_prompt_q = prompt_grad_q.reshape(1, prompt_rows, HEADS * HEAD_DIM).astype(jnp.bfloat16)
    grad_prompt_kv = (self_grads + returned)[None].astype(jnp.bfloat16)
    return (grad_prompt_q, grad_prompt_kv, grad_resp_q, grad_resp_kv)


def solution(mesh):
    in_specs = (
        P("resp", "ctx", None),
        P("resp", "ctx", None),
        P("resp", "ctx", None),
        P("resp", None, None),
        P("resp", None, None),
        P("resp", None, None),
        P("resp", None),
        P("resp", None),
        P("resp"),
    )
    out_specs = (
        P("resp", "ctx", None),
        P("resp", "ctx", None),
        P("resp", None, None),
        P("resp", None, None),
    )
    return jax.shard_map(body, mesh=mesh, in_specs=in_specs, out_specs=out_specs, check_vma=False)
```

profile of v0, /device:TPU:1, one launch (start us, length us, event | category | flops | bytes accessed | tf_op | source)
XLA Modules:
  0.0 647.6 jit_solution(13083271034718954800)
XLA Ops:
  11.8 3.6 copy.148
  19.6 84.8 %all-reduce = (f32[32]{0:T(128)S(1)}, f32[32]{0:T(128)S(1)}, f32[32]{0:T(128)S(1)}) all-reduce(f32[32]{0:T(128)S(1)} %get-tuple-element.143, f32[32]{0:T(128)S(1)} %get-tuple-element.142, f32[32]{0:T(128)S(1)} %get-tuple-element.141), channel_id=1, replica_groups=mesh['ctx'=4,'resp'=32] {'resp'}, use_global_device_ids=true, to_apply=%region_11.12 | all-reduce | flops 96 | bytes 768 | tf_op jit(solution)/shard_map/psum | solution.py:141
  105.0 3.4 fusion.100
  111.1 5.2 fusion.5
  116.3 5.1 exponential_reduce_fusion
  122.8 8.5 %fusion.19 = f32[192,4,8]{0,2,1:T(8,128)S(1)} fusion(f32[1,192,4,8,128]{4,3,2,0,1:T(8,128)} %bitcast.255, bf16[768,4,128,1]{0,2,3,1:T(8,128)(2,1)} %bitcast.264, f32[4,768,192,8]{1,2,3,0:T(8,128)S(1)} %get-tuple-element.170, f32[4,8,192]{2,1,0:T(8,128)S(1)} %log_add_fusion.1, pred[192,768]{1,0:T(8,128)(4,1)S(1)} %iota_compare_fusion), kind=kOutput, calls=%fused_computation.37 | convolution fusion | flops 1228400640 | bytes 23003136 | tf_op jit(solution)/shard_map/rkglm,rmkd->rlkgd/dot_general | solution.py:64
  131.3 13.7 %fusion.7 = bf16[4,8,192,768]{3,2,1,0:T(8,128)(2,1)} fusion(f32[4,768,192,8]{1,2,3,0:T(8,128)} %copy-done.3, f32[4,8,192]{2,1,0:T(8,128)S(1)} %bitcast.275, f32[4,8,192]{2,1,0:T(8,128)S(1)} %log_add_fusion.1, pred[192,768]{1,0:T(8,128)(4,1)S(1)} %iota_compare_fusion, bf16[768,4,128,1]{0,2,3,1:T(8,128)(2,1)} %bitcast.265, bf16[192,4,8,128]{3,2,1,0:T(8,128)(2,1)} %bitcast.260), kind=kOutput, calls=%fused_computation.15 | convolution fusion | flops 1236271104 | bytes 30867456 | tf_op jit(solution)/shard_map/rlkgd,rmkd->rkglm/dot_general | solution.py:77
  145.0 26.4 %all-gather.6.cloned.1.call-done = bf16[32,192,1024]{2,1,0:T(8,128)(2,1)} async-done(((bf16[1,192,1024]{2,1,0:T(8,128)(2,1)}), bf16[32,192,1024]{2,1,0:T(8,128)(2,1)}) %all-gather.6.cloned.1.call-update) | async-done | bytes 12582928 | tf_op jit(solution)/shard_map/all_gather | solution.py:159
  171.4 6.4 gather_fusion
  184.3 6.7 %all-gather.1 = f32[16,4,8,64]{3,2,1,0:T(8,128)S(1)} all-gather(f32[4,4,8,64]{3,2,1,0:T(8,128)S(1)} %max.30), channel_id=3, replica_groups=mesh['ctx'=4,'resp'=32] {'ctx'}, dimensions={0}, use_global_device_ids=true | all-gather | bytes 163840 | tf_op jit(solution)/shard_map/all_gather | solution.py:15
  194.1 5.9 all-gather.2
  200.2 5.6 fusion.13
  206.3 3.7 fusion.75
  212.5 6.9 %fusion.29 = bf16[4,768,128]{1,2,0:T(8,128)(2,1)} fusion(bf16[4,8,192,768]{3,2,1,0:T(8,128)(2,1)} %fusion.7, bf16[192,4,8,128]{3,2,1,0:T(8,128)(2,1)S(1)} %bitcast.245), kind=kOutput, calls=%fused_computation.53 | convolution fusion | flops 1208745984 | bytes 11796480 | tf_op jit(solution)/shard_map/rkglm,rlkgd->rmkd/dot_general | solution.py:89
  220.8 11.1 %bitcast_convert_fusion = bf16[4,768,128]{1,2,0:T(8,128)(2,1)} fusion(bf16[192,4,8,128]{3,2,1,0:T(8,128)(2,1)} %bitcast.261, f32[4,768,192,8]{1,2,3,0:T(8,128)} %copy-done.3, f32[4,8,192]{2,1,0:T(8,128)S(1)} %log_add_fusion.1, pred[192,768]{1,0:T(8,128)(4,1)S(1)} %iota_compare_fusion), kind=kOutput, calls=%fused_computation.51 | convolution fusion | flops 1227227136 | bytes 21405696 | tf_op jit(solution)/shard_map/rkglm,rlkgd->rmkd/dot_general | solution.py:92
  242.5 3.4 reshape.300
  245.9 21.6 %all-reduce.5.cloned.1.call-done = bf16[4,64,4,8,128]{4,1,3,2,0:T(8,128)(2,1)} async-done(((bf16[4,64,4,8,128]{4,1,3,2,0:T(8,128)(2,1)}), bf16[4,64,4,8,128]{4,1,3,2,0:T(8,128)(2,1)}) %all-reduce.5.cloned.1.call-update) | async-done | bytes 2097168 | tf_op jit(solution)/shard_map/psum | solution.py:179
  270.4 5.9 fusion.9
  283.5 12.4 %convolution_convert_fusion = bf16[32,192,1024]{2,0,1:T(8,128)(2,1)S(1)} fusion(f32[4,192,512]{2,0,1:T(4,128)} %reshape.300, f32[4,192,512]{2,0,1:T(4,128)} %reshape.299, s32[4]{0:T(128)S(1)} %bitcast.274), kind=kOutput, calls=%fused_computation.26 | convolution fusion | flops 309067904 | bytes 15728656 | tf_op jit(solution)/shard_map/rp,rmx->pmx/dot_general | solution.py:221
  295.9 21.5 %copy.89 = bf16[32,192,1024]{2,1,0:T(8,128)(2,1)} copy(bf16[32,192,1024]{2,0,1:T(8,128)(2,1)S(1)} %convolution_convert_fusion) | data formatting | bytes 25165824 | tf_op jit(solution)/shard_map/convert_element_type | solution.py:223
  330.3 4.2 convert_element_type.136
  336.2 6.4 fusion.35
  345.7 222.5 %reduce-scatter.5.cloned.1.call-done = bf16[1,192,1024]{2,1,0:T(8,128)(2,1)} async-done(((bf16[32,192,1024]{2,1,0:T(8,128)(2,1)}), bf16[1,192,1024]{2,1,0:T(8,128)(2,1)}) %reduce-scatter.5.cloned.1.call-update) | async-done | bytes 393232 | tf_op jit(solution)/shard_map/reduce_scatter | solution.py:222
  570.2 66.4 %all-reduce.7.cloned.1.call-done = (bf16[4,64,4096]{2,1,0:T(8,128)(2,1)}, bf16[4,64,1024]{2,1,0:T(8,128)(2,1)}) async-done(((bf16[4,64,4096]{2,1,0:T(8,128)(2,1)}, bf16[4,64,1024]{2,1,0:T(8,128)(2,1)}), (bf16[4,64,4096]{2,1,0:T(8,128)(2,1)}, bf16[4,64,1024]{2,1,0:T(8,128)(2,1)})) %all-reduce.7.cloned.1.call-update) | async-done | bytes 2621456 | tf_op jit(solution)/shard_map/psum | solution.py:206
  (139 shorter events, 71.6 us)
Async XLA Ops:
  7.2 97.2 %copy-start = (s32[4,64]{1,0:T(4,128)S(1)}, s32[4,64]{1,0:T(4,128)}, u32[]{:S(2)}) copy-start(s32[4,64]{1,0:T(4,128)} %param.18) | copy-start | bytes 3076
  7.2 4.6 copy-start.28
  7.2 101.2 %all-gather.8.cloned.1.call-start = ((), (), s32[]{:S(2)}) async-start(), calls=%async_computation.6 | async-start | bytes 1966080 | tf_op jit(solution)/shard_map/all_gather | solution.py:109
  7.9 163.5 %all-gather.6.cloned.1.call-start = ((), (), s32[]{:S(2)}) async-start(), calls=%async_computation.3 | async-start | bytes 12976128 | tf_op jit(solution)/shard_map/all_gather | solution.py:159
  8.7 258.8 %all-reduce.5.cloned.1.call-start = ((), (), s32[]{:S(2)}) async-start(), calls=%async_computation.4 | async-start | bytes 4194304 | tf_op jit(solution)/shard_map/psum | solution.py:179
  11.7 93.3 %copy-start.7 = (bf16[32,8,32,128]{3,2,1,0:T(8,128)(2,1)}, bf16[32,8,32,128]{3,2,1,0:T(8,128)(2,1)S(1)}, u32[]{:S(2)}) copy-start(bf16[32,8,32,128]{3,2,1,0:T(8,128)(2,1)S(1)} %copy.151) | copy-start | bytes 6291460
  111.1 5.2 copy-start.13
  116.3 6.5 %copy-start.3 = (f32[4,768,192,8]{1,2,3,0:T(8,128)}, f32[4,768,192,8]{1,2,3,0:T(8,128)S(1)}, u32[]{:S(2)}) copy-start(f32[4,768,192,8]{1,2,3,0:T(8,128)S(1)} %get-tuple-element.170) | copy-start | bytes 56623108
  145.0 36.3 %copy-start.8 = (bf16[32,8,32,128]{3,2,1,0:T(8,128)(2,1)S(1)}, bf16[32,8,32,128]{3,2,1,0:T(8,128)(2,1)}, u32[]{:S(2)}) copy-start(bf16[32,8,32,128]{3,2,1,0:T(8,128)(2,1)} %copy-done.7) | copy-start | bytes 6291460
  181.4 9.7 %copy-start.11 = (f32[4,4,8,64,16]{3,4,2,1,0:T(8,128)S(1)}, f32[4,4,8,64,16]{3,4,2,1,0:T(8,128)}, u32[]{:S(2)}) copy-start(f32[4,4,8,64,16]{3,4,2,1,0:T(8,128)} %get-tuple-element.174) | copy-start | bytes 1572868
  184.3 9.7 %copy-start.2 = (f32[4,4,192,64,8]{2,3,4,1,0:T(8,128)}, f32[4,4,192,64,8]{2,3,4,1,0:T(8,128)S(1)}, u32[]{:S(2)}) copy-start(f32[4,4,192,64,8]{2,3,4,1,0:T(8,128)S(1)} %get-tuple-element.172) | copy-start | bytes 18874372
  200.2 5.8 copy-start.20
  206.0 4.0 copy-start.19
  206.3 3.7 copy-start.16
  212.2 133.5 %reduce-scatter.3.cloned.1.call-start = ((), (), s32[]{:S(2)}) async-start(), calls=%async_computation.2 | async-start | bytes 1966080 | tf_op jit(solution)/shard_map/reduce_scatter | solution.py:133
  234.7 333.4 %reduce-scatter.5.cloned.1.call-start = ((), (), s32[]{:S(2)}) async-start(), calls=%async_computation.5 | async-start | bytes 12976128 | tf_op jit(solution)/shard_map/reduce_scatter | solution.py:222
  270.4 5.9 copy-start.9
  317.4 319.1 %all-reduce.7.cloned.1.call-start = ((), (), s32[]{:S(2)}) async-start(), calls=%async_computation.7 | async-start | bytes 5242880 | tf_op jit(solution)/shard_map/psum | solution.py:206
  320.5 4.9 copy-start.6
  320.5 4.9 copy-start.15
  327.6 6.9 %copy-start.10 = (bf16[32,8,32,128]{3,2,1,0:T(8,128)(2,1)S(1)}, bf16[32,8,32,128]{3,2,1,0:T(8,128)(2,1)}, u32[]{:S(2)}) copy-start(bf16[32,8,32,128]{3,2,1,0:T(8,128)(2,1)} %copy-done.7) | copy-start | bytes 6291460
  327.6 6.9 %copy-start.23 = (bf16[4,4,8,64,16]{3,4,2,1,0:T(8,128)(2,1)S(1)}, bf16[4,4,8,64,16]{3,4,2,1,0:T(8,128)(2,1)}, u32[]{:S(2)}) copy-start(bf16[4,4,8,64,16]{3,4,2,1,0:T(8,128)(2,1)} %copy-done.22) | copy-start | bytes 786436
  330.3 4.9 copy-start.25
  342.6 297.9 %copy-start.1 = (s32[4,64]{1,0:T(4,128)S(1)}, s32[4,64]{1,0:T(4,128)}, u32[]{:S(2)}) copy-start(s32[4,64]{1,0:T(4,128)} %param.18) | copy-start | bytes 3076
  (11 other events, 27.4 us)
Sparse Core Ops, SparseCore 0:
  9.7 28.6 all-gather.7
  41.5 129.9 all-gather.5
  212.3 55.1 all-reduce.4
  269.9 24.8 reduce-scatter.2
  317.5 250.6 reduce-scatter.4
  571.2 65.3 all-reduce.6
where the time goes:
time: 656 us; the launch traced here: 648 us
  waiting for transfers between devices  338 us (52%)
  blocking collectives  97.4 us (15%)
  matrix products  94.2 us (14%)
  local copies, waits for them, and re-layouts  78.7 us (12%)
  other arithmetic  23.6 us (4%)
  between operations  14.9 us (2%)
    reduce_scatter x1, waiting for transfers between devices, body(): lax.psum_scatter(per_prompt.astype(jnp.bfloat16), 'resp', scatter_dimensi...  222 us
    psum x1, blocking collectives, body(): lax.psum((jnp.sum(onehot, axis=0), jnp.sum(onehot * reward_values[:, None...  84.8 us
    psum x1, waiting for transfers between devices, body(): lax.psum(grad_query.reshape(responses_here, resp_length, HEADS * HEAD_DIM...  66.4 us
    all_gather x1, waiting for transfers between devices, body(): tiles = lax.all_gather(prompt_kv, 'resp', axis=0, tiled=True)  26.4 us
    psum x1, waiting for transfers between devices, sum_output(): return lax.psum(output.astype(jnp.bfloat16), 'ctx').astype(jnp.float32)  21.6 us
    convert_element_type x1, local copies, waits for them, and re-layouts, body(): per_prompt.astype(jnp.bfloat16)  21.5 us
    dot_general x3, matrix products, attend(): jnp.einsum('rlkgd,rmkd->rkglm', cotangent, entry[1], preferred_element_ty...  21.4 us
    dot_general x3, matrix products, attend(): jnp.einsum('rkglm,rlkgd->rmkd', narrow_weight, cotangent, preferred_eleme...  16.9 us
  transfers between devices with their start and end apart: 6, of which 4 were waited for; matrix products, arithmetic and copies ran while one was open for 25% of the time, Pallas kernels for 0%

commit v1 on v0

v1 whole, which is shorter than its diff:
```python
import functools
import math

import jax
import jax.numpy as jnp
from jax import lax
from jax.experimental import pallas as pl
from jax.experimental.pallas import tpu as pltpu
from jax.sharding import PartitionSpec as P

MESH = pl.DeviceIdType.MESH
KV_HEADS = 4
HEAD_DIM = 128
CTX = 4
ROUTE_ROW = 4
REWARD_ROW = 5


def dot_nt(a, b):
    return lax.dot_general(a, b, (((1,), (1,)), ((), ())), preferred_element_type=jnp.float32)


def dot_tn(a, b):
    return lax.dot_general(a, b, (((0,), (0,)), ((), ())), preferred_element_type=jnp.float32)


def dot_nn(a, b):
    return lax.dot_general(a, b, (((1,), (0,)), ((), ())), preferred_element_type=jnp.float32)


def aligned(start, size):
    return pl.ds(pl.multiple_of(start, 16), size)


def columns(start, size):
    return pl.ds(pl.multiple_of(start, 128), size)


def attention_grads(queries, cotangent, pieces, scale):
    to_power = scale * math.log2(math.e)
    scores = []
    for keys, values, adjust in pieces:
        part = dot_nt(keys, queries) * to_power
        scores.append(part if adjust is None else adjust(part))
    highest = functools.reduce(
        jnp.maximum, [jnp.max(part, axis=0, keepdims=True) for part in scores]
    )
    powers = [jnp.exp2(part - highest) for part in scores]
    total = functools.reduce(jnp.add, [jnp.sum(part, axis=0, keepdims=True) for part in powers])
    inverse = 1.0 / total
    grad_probs = [dot_nt(values, cotangent) for keys, values, adjust in pieces]
    delta = inverse * functools.reduce(
        jnp.add,
        [jnp.sum(a * b, axis=0, keepdims=True) for a, b in zip(powers, grad_probs)],
    )
    grad_query = None
    grads = []
    for (keys, values, adjust), power, grad_prob in zip(pieces, powers, grad_probs):
        weight = power * inverse
        narrow = weight.astype(jnp.bfloat16)
        grad_score = (weight * (grad_prob - delta)).astype(jnp.bfloat16)
        grad_values = dot_nn(narrow, cotangent)
        grad_keys = dot_nn(grad_score, queries)
        term = dot_tn(keys, grad_score)
        grad_query = term if grad_query is None else grad_query + term
        grads.append((grad_keys, grad_values))
    return grad_query, grads


def kernel(
    ring,
    routes_in,
    rewards_in,
    tree_in,
    pq,
    pkv,
    pcot,
    rq,
    rkv,
    rcot,
    dpq,
    dpkv,
    drq,
    drkv,
    pq_v,
    pcot_v,
    tiles,
    rq_v,
    rcot_v,
    tree_k,
    tree_v,
    notes,
    picks_v,
    picks,
    pieces_in,
    picked,
    chosen,
    bias,
    self_acc,
    self_out,
    self_in,
    dpq_v,
    grads,
    shares,
    share_acc,
    totals,
    returned,
    drq_v,
    dtree_k,
    dtree_v,
    sem_load,
    sem_note,
    sem_piece,
    sem_tile_send,
    sem_tile_recv,
    sem_pick_send,
    sem_pick_recv,
    sem_self_send,
    sem_self_recv,
    sem_share_send,
    sem_share_recv,
    sem_query,
    sem_tree,
    sem_total,
):
    scale = 1.0 / math.sqrt(HEAD_DIM)
    c = lax.axis_index("ctx")
    me = lax.axis_index("resp")
    rows = pq.shape[0]
    length = CTX * rows
    count, tokens = rq.shape[0], rq.shape[1]
    group = pq.shape[1] // (KV_HEADS * HEAD_DIM)
    width = group * HEAD_DIM
    half = KV_HEADS * HEAD_DIM
    size = 2 * length // ring
    blocks = rows // size
    source = lax.rem(me, ring // 2) // blocks
    own_block = lax.rem(me, blocks)
    own_kind = me // (ring // 2)
    beside = c + 1 - 2 * lax.rem(c, 2)
    across = lax.rem(c + 2, CTX)
    x_size = min(4, ring)
    y_size = min(4, ring // x_size)
    z_size = ring // (x_size * y_size)

    def moved(step):
        x = lax.rem(lax.rem(me, x_size) + lax.rem(step, x_size), x_size)
        y = lax.rem(lax.rem(me // x_size, y_size) + lax.rem(step // x_size, y_size), y_size)
        z = lax.rem(me // (x_size * y_size) + step // (x_size * y_size), z_size)
        return (z * y_size + y) * x_size + x

    def remote(src, dst, send, recv, where):
        return pltpu.make_async_remote_copy(
            src_ref=src,
            dst_ref=dst,
            send_sem=send,
            recv_sem=recv,
            device_id=where,
            device_id_type=MESH,
        )

    def settle(ref, sem):
        pltpu.make_async_copy(ref, ref, sem).wait()

    own_columns = columns(c * width, width)
    loads = [
        pltpu.make_async_copy(pq, pq_v, sem_load.at[0]),
        pltpu.make_async_copy(pcot, pcot_v, sem_load.at[1]),
        pltpu.make_async_copy(pkv, tiles.at[aligned(c * rows, rows)], sem_load.at[2]),
        pltpu.make_async_copy(rq.at[:, :, own_columns], rq_v, sem_load.at[3]),
        pltpu.make_async_copy(rcot.at[:, :, own_columns], rcot_v, sem_load.at[4]),
        pltpu.make_async_copy(
            rkv.at[:, :, columns(c * HEAD_DIM, HEAD_DIM)], tree_k, sem_load.at[5]
        ),
        pltpu.make_async_copy(
            rkv.at[:, :, columns(half + c * HEAD_DIM, HEAD_DIM)], tree_v, sem_load.at[6]
        ),
    ]
    for load in loads:
        load.start()

    barrier = pltpu.get_barrier_semaphore()

    def greet(step, carry):
        there = (lax.rem(c + step // ring, CTX), lax.rem(me + lax.rem(step, ring), ring))
        pl.semaphore_signal(barrier, inc=1, device_id=there, device_id_type=MESH)
        return carry

    lax.fori_loop(1, CTX * ring, greet, 0)

    row = lax.broadcasted_iota(jnp.int32, (8, 128), 0)
    lane = lax.broadcasted_iota(jnp.int32, (8, 128), 1)
    note = jnp.zeros((8, 128), jnp.int32)
    inside = lane // 16 == lax.rem(me, 8)
    for r in range(count):
        route = routes_in[r, 0]
        note = jnp.where((row == r) & inside, route * 16 + lane % 16, note)
        note = jnp.where((row == ROUTE_ROW) & (lane == r), route, note)
        note = jnp.where((row == REWARD_ROW) & (lane == r), rewards_in[r], note)
    notes[me] = note

    pl.semaphore_wait(barrier, CTX * ring - 1)

    def send_note(step, carry):
        there = moved(step)
        remote(notes.at[me], notes.at[me], sem_note.at[0], sem_note.at[1], (c, there)).start()
        return carry

    lax.fori_loop(1, ring, send_note, 0)

    def send_piece(step, carry):
        head = lax.rem(c + step, KV_HEADS)
        part = lax.rem(step // KV_HEADS + me, 2 * blocks)
        kind = part // blocks
        block = lax.rem(part, blocks)
        there = kind * (ring // 2) + c * blocks + block
        piece = pkv.at[
            aligned(block * size, size), columns(kind * half + head * HEAD_DIM, HEAD_DIM)
        ]
        here = (head == c) & (there == me)

        @pl.when(here)
        def _():
            pltpu.make_async_copy(piece, pieces_in.at[me], sem_piece.at[2]).start()

        @pl.when(jnp.logical_not(here))
        def _():
            remote(
                piece, pieces_in.at[me], sem_piece.at[0], sem_piece.at[1], (head, there)
            ).start()

        return carry

    lax.fori_loop(0, KV_HEADS * 2 * blocks, send_piece, 0)

    def tile(index):
        return tiles.at[pl.ds(index * rows, rows)]

    def send_tile(src, index, slot, where):
        return remote(src, tile(index), sem_tile_send.at[slot], sem_tile_recv.at[index], (where, me))

    @pl.when(c == 0)
    def _():
        send_tile(pkv, 0, 0, 2).start()
        send_tile(pkv, 0, 1, 1).start()

    @pl.when(c == 1)
    def _():
        send_tile(pkv, 1, 0, 3).start()

    @pl.when(c == 2)
    def _():
        send_tile(pkv, 2, 0, 3).start()

    for index in range(1, CTX):

        @pl.when(c < index)
        def _():
            tiles[index * rows : (index + 1) * rows, :] = jnp.zeros((rows, 2 * half), jnp.bfloat16)

    position = lax.broadcasted_iota(jnp.int32, (length, 2 * rows), 0)
    query = lax.broadcasted_iota(jnp.int32, (length, 2 * rows), 1)
    query = jnp.where(query >= rows, query - rows, query) + c * rows
    bias[...] = jnp.where(position <= query, 0.0, -jnp.inf)
    self_acc[...] = jnp.zeros_like(self_acc)

    settle(notes.at[pl.ds(0, ring - 1)], sem_note.at[1])
    every = notes[...]
    note_row = lax.broadcasted_iota(jnp.int32, every.shape, 1)
    routes = jnp.sum(jnp.where(note_row == ROUTE_ROW, every, 0), axis=1)
    rewards = jnp.sum(jnp.where(note_row == REWARD_ROW, every, 0), axis=1).astype(jnp.float32)
    picks_v[...] = routes
    to_scalars = pltpu.make_async_copy(picks_v, picks, sem_note.at[2])
    to_scalars.start()
    to_scalars.wait()

    @pl.when(c == source)
    def _():
        settle(pieces_in.at[me], sem_piece.at[2])
        settle(pieces_in.at[pl.ds(0, ring - 1)], sem_piece.at[1])

    @pl.when(c != source)
    def _():
        settle(pieces_in, sem_piece.at[1])

    for r in range(count):
        chosen[r, aligned(me * size, size), :] = pieces_in[picks[me, r]]

    def send_pick(step, carry):
        r = step // (ring - 1)
        there = moved(lax.rem(step, ring - 1) + 1)
        picked[r, there] = pieces_in[picks[there, r]]
        remote(
            picked.at[r, there],
            chosen.at[r, aligned(me * size, size)],
            sem_pick_send.at[r],
            sem_pick_recv.at[r],
            (c, there),
        ).start()
        return carry

    lax.fori_loop(0, count * (ring - 1), send_pick, 0)

    @pl.when(c == 2)
    def _():
        settle(tile(0), sem_tile_recv.at[0])
        send_tile(tile(0), 0, 1, 3).start()
        settle(tile(1), sem_tile_recv.at[1])

    @pl.when(c == 3)
    def _():
        settle(tile(1), sem_tile_recv.at[1])
        send_tile(tile(1), 1, 0, 2).start()
        settle(tile(0), sem_tile_recv.at[0])
        settle(tile(2), sem_tile_recv.at[2])

    @pl.when(c == 1)
    def _():
        settle(tile(0), sem_tile_recv.at[0])

    for load in loads:
        load.wait()

    note_lane = lax.broadcasted_iota(jnp.int32, routes.shape, 1)
    for r in range(count):
        same = ((routes == routes_in[r, 0]) & (note_lane < count)).astype(jnp.float32)

        def summed(values):
            return jnp.sum(jnp.sum(values, axis=1, keepdims=True), axis=0, keepdims=True)

        number = summed(same)
        reward_sum = summed(same * rewards)
        reward_square = summed(same * rewards * rewards)
        variance = reward_square * number - reward_sum * reward_sum
        spread = jnp.sqrt(jnp.maximum(variance, number * number)) / number
        own_reward = jnp.full((1, 1), rewards_in[r], jnp.int32).astype(jnp.float32)
        advantage = (own_reward - reward_sum / number) / spread
        rcot_v[r] = (advantage * rcot_v[r].astype(jnp.float32)).astype(jnp.bfloat16)

    def prompt_step(step, carry):
        head = step // (group // 2)
        first = columns(step * 2 * HEAD_DIM, HEAD_DIM)
        second = columns(step * 2 * HEAD_DIM + HEAD_DIM, HEAD_DIM)
        key_columns = columns(head * HEAD_DIM, HEAD_DIM)
        value_columns = columns(half + head * HEAD_DIM, HEAD_DIM)
        queries = jnp.concatenate([pq_v[:, first], pq_v[:, second]], axis=0)
        cotangent = jnp.concatenate([pcot_v[:, first], pcot_v[:, second]], axis=0)
        grad_query, ((grad_keys, grad_values),) = attention_grads(
            queries,
            cotangent,
            [(tiles[:, key_columns], tiles[:, value_columns], lambda part: part + bias[...])],
            scale,
        )
        self_acc[:, key_columns] += grad_keys
        self_acc[:, value_columns] += grad_values
        turned = jnp.transpose(grad_query * scale).astype(jnp.bfloat16)
        dpq_v[:, first] = turned[:rows]
        dpq_v[:, second] = turned[rows:]
        return carry

    lax.fori_loop(0, KV_HEADS * group // 2, prompt_step, 0)
    store_dpq = pltpu.make_async_copy(dpq_v, dpq, sem_load.at[7])
    store_dpq.start()
    self_acc[:, :half] = self_acc[:, :half] * scale

    def self_tile(index):
        return self_acc[index * rows : (index + 1) * rows, :]

    def send_self(values, slot, there, there_slot):
        self_out[slot] = values.astype(jnp.bfloat16)
        remote(
            self_out.at[slot],
            self_in.at[there_slot],
            sem_self_send.at[slot],
            sem_self_recv.at[there_slot],
            (there, me),
        ).start()

    @pl.when(c == 1)
    def _():
        send_self(self_tile(0), 0, 0, 0)

    @pl.when(c == 2)
    def _():
        send_self(self_tile(1), 0, 3, 0)

    @pl.when(c == 3)
    def _():
        send_self(self_tile(0), 0, 2, 0)
        send_self(self_tile(2), 1, 2, 1)

    key_place = lax.broadcasted_iota(jnp.int32, (tokens, group * tokens), 0)
    query_place = lax.broadcasted_iota(jnp.int32, (tokens, group * tokens), 1) % tokens
    square_row = lax.broadcasted_iota(jnp.int32, (tokens, tokens), 0)
    square_column = lax.broadcasted_iota(jnp.int32, (tokens, tokens), 1)

    def stacked(values):
        return jnp.concatenate(
            [values[:, g * HEAD_DIM : (g + 1) * HEAD_DIM] for g in range(group)], axis=0
        )

    def query_rows(r, owner):
        return drq.at[r, :, columns(owner * width, width)]

    def response_step(r, carry):
        settle(chosen.at[r, pl.ds(0, (ring - 1) * size)], sem_pick_recv.at[r])
        ends = tree_in[pl.ds(r, 1), :]
        ends = jnp.sum(
            jnp.where(square_row == square_column, ends, 0), axis=1, keepdims=True
        )
        allowed = (key_place <= query_place) & (query_place < ends)
        queries = stacked(rq_v[r])
        cotangent = stacked(rcot_v[r])
        grad_query, (prompt_terms, tree_terms) = attention_grads(
            queries,
            cotangent,
            [
                (chosen[r, :length, :], chosen[r, length:, :], None),
                (tree_k[r], tree_v[r], lambda part: jnp.where(allowed, part, -jnp.inf)),
            ],
            scale,
        )
        grads[r, :length, :] = (prompt_terms[0] * scale).astype(jnp.bfloat16)
        grads[r, length:, :] = prompt_terms[1].astype(jnp.bfloat16)
        dtree_k[r] = (tree_terms[0] * scale).astype(jnp.bfloat16)
        dtree_v[r] = tree_terms[1].astype(jnp.bfloat16)
        turned = jnp.transpose(grad_query * scale).astype(jnp.bfloat16)
        drq_v[r] = jnp.concatenate(
            [turned[g * tokens : (g + 1) * tokens] for g in range(group)], axis=1
        )

        def send_share(step, inner):
            there = moved(step)
            remote(
                grads.at[r, aligned(there * size, size)],
                shares.at[r, me],
                sem_share_send.at[r],
                sem_share_recv.at[r],
                (c, there),
            ).start()
            return inner

        mine = query_rows(r, c)
        remote(drq_v.at[r], mine, sem_query.at[0, r], sem_query.at[1, r], (across, me)).start()
        lax.fori_loop(1, ring, send_share, 0)
        shares[r, me] = grads[r, aligned(me * size, size), :]
        remote(drq_v.at[r], mine, sem_query.at[2, r], sem_query.at[3, r], (beside, me)).start()
        pltpu.make_async_copy(drq_v.at[r], mine, sem_query.at[6, r]).start()
        return carry

    lax.fori_loop(0, count, response_step, 0)

    def tree_part(kind, owner):
        return drkv.at[:, :, columns(kind * half + owner * HEAD_DIM, HEAD_DIM)]

    tree_copies = []
    for kind, values in ((0, dtree_k), (1, dtree_v)):
        mine = tree_part(kind, c)
        tree_copies.append(
            (
                remote(values, mine, sem_tree.at[0, kind], sem_tree.at[1, kind], (across, me)),
                remote(values, mine, sem_tree.at[2, kind], sem_tree.at[3, kind], (beside, me)),
                pltpu.make_async_copy(values, mine, sem_tree.at[6, kind]),
            )
        )
        for copy in tree_copies[-1]:
            copy.start()

    @pl.when(c == 2)
    def _():
        settle(self_in.at[0], sem_self_recv.at[0])
        send_self(self_tile(0) + self_in[0].astype(jnp.float32), 2, 0, 2)

    @pl.when(c == 3)
    def _():
        settle(self_in.at[0], sem_self_recv.at[0])
        send_self(self_tile(1) + self_in[0].astype(jnp.float32), 2, 1, 2)

    subs = size // 16
    share_acc[...] = jnp.zeros_like(share_acc)
    groups = ring // 8

    def share_step(r, carry):
        settle(query_rows(r, across), sem_query.at[1, r])
        theirs = query_rows(r, across)
        remote(theirs, theirs, sem_query.at[4, r], sem_query.at[5, r], (beside, me)).start()
        target = lax.broadcasted_iota(jnp.int32, (ring * 16, 128), 0)
        codes = jnp.sum(
            jnp.where(note_row == r, notes[...], 0).reshape(groups, 8, 8, 128), axis=1
        )
        codes = jnp.sum(codes, axis=1)
        spread = jnp.concatenate(
            [
                (target == codes[g : g + 1, :]).astype(jnp.float32).astype(jnp.bfloat16)
                for g in range(groups)
            ],
            axis=1,
        )
        settle(shares.at[r, pl.ds(0, ring - 1)], sem_share_recv.at[r])
        for s in range(subs):
            part = shares[r, :, s * 16 : (s + 1) * 16, :].reshape(ring * 16, HEAD_DIM)
            share_acc[s] += dot_nn(spread, part)
        return carry

    lax.fori_loop(0, count, share_step, 0)
    for s in range(subs):
        totals[:, s * 16 : (s + 1) * 16, :] = (
            share_acc[s].reshape(ring, 16, HEAD_DIM).astype(jnp.bfloat16)
        )

    home = returned.at[
        aligned(own_block * size, size), columns(own_kind * half + c * HEAD_DIM, HEAD_DIM)
    ]

    @pl.when(c == source)
    def _():
        pltpu.make_async_copy(totals.at[me], home, sem_total.at[2]).start()

    @pl.when(c != source)
    def _():
        remote(totals.at[me], home, sem_total.at[0], sem_total.at[1], (source, me)).start()

    def send_total(step, carry):
        there = moved(step)
        remote(
            totals.at[there], home, sem_total.at[0], sem_total.at[1], (source, there)
        ).start()
        return carry

    lax.fori_loop(1, ring, send_total, 0)

    def add_self(slot):
        settle(self_in.at[slot], sem_self_recv.at[slot])
        return self_in[slot].astype(jnp.float32)

    own_rows = pl.ds(pl.multiple_of(c * rows, rows), rows)

    @pl.when(c == 0)
    def _():
        self_acc[own_rows, :] += add_self(0) + add_self(2)

    @pl.when(c == 1)
    def _():
        self_acc[own_rows, :] += add_self(2)

    @pl.when(c == 2)
    def _():
        self_acc[own_rows, :] += add_self(1)

    settle(notes.at[pl.ds(0, ring - 1)], sem_note.at[0])

    @pl.when(c == source)
    def _():
        settle(pieces_in.at[pl.ds(0, ring - 1)], sem_piece.at[0])

    @pl.when(c != source)
    def _():
        settle(pieces_in, sem_piece.at[0])

    @pl.when(c == 0)
    def _():
        send_tile(pkv, 0, 0, 2).wait_send()
        send_tile(pkv, 0, 1, 1).wait_send()

    @pl.when(c == 1)
    def _():
        send_tile(pkv, 1, 0, 3).wait_send()

    @pl.when(c == 2)
    def _():
        send_tile(pkv, 2, 0, 3).wait_send()
        send_tile(tile(0), 0, 1, 3).wait_send()

    @pl.when(c == 3)
    def _():
        send_tile(tile(1), 1, 0, 2).wait_send()

    @pl.when(c >= 1)
    def _():
        settle(self_out.at[0], sem_self_send.at[0])

    @pl.when(c == 3)
    def _():
        settle(self_out.at[1], sem_self_send.at[1])

    @pl.when(c >= 2)
    def _():
        settle(self_out.at[2], sem_self_send.at[2])

    for kind in range(2):
        settle(tree_part(kind, across), sem_tree.at[1, kind])
        theirs = tree_part(kind, across)
        remote(theirs, theirs, sem_tree.at[4, kind], sem_tree.at[5, kind], (beside, me)).start()
    for r in range(count):
        settle(picked.at[r, pl.ds(0, ring - 1)], sem_pick_send.at[r])
        settle(shares.at[r, pl.ds(0, ring - 1)], sem_share_send.at[r])
        for slot in (0, 2, 3, 4, 5, 6):
            settle(drq_v.at[r], sem_query.at[slot, r])
    for kind, values in ((0, dtree_k), (1, dtree_v)):
        for slot in (0, 2, 3, 4, 5, 6):
            settle(values, sem_tree.at[slot, kind])
    store_dpq.wait()

    @pl.when(c == source)
    def _():
        settle(totals.at[me], sem_total.at[2])
        settle(totals.at[pl.ds(0, ring - 1)], sem_total.at[0])
        settle(totals.at[pl.ds(0, ring - 1)], sem_total.at[1])

    @pl.when(c != source)
    def _():
        settle(totals, sem_total.at[0])
        settle(totals, sem_total.at[1])

    dpkv[...] = (self_acc[own_rows, :] + returned[...].astype(jnp.float32)).astype(jnp.bfloat16)


def body(
    prompt_q, prompt_kv, prompt_cot, resp_q, resp_kv, resp_cot, resp_prompt, tree_end, rewards
):
    ring = lax.axis_size("resp")
    rows, wide = prompt_q.shape[1:]
    kv_wide = prompt_kv.shape[2]
    count, tokens = resp_q.shape[:2]
    length = CTX * rows
    group = wide // (KV_HEADS * HEAD_DIM)
    width = group * HEAD_DIM
    size = 2 * length // ring
    bf16, f32, i32 = jnp.bfloat16, jnp.float32, jnp.int32
    any_space = pl.BlockSpec(memory_space=pl.ANY)
    scalars = pl.BlockSpec(memory_space=pltpu.SMEM)
    vector = pl.BlockSpec(memory_space=pltpu.VMEM)
    dma = pltpu.SemaphoreType.DMA
    dpq, dpkv, drq, drkv = pl.pallas_call(
        functools.partial(kernel, ring),
        out_shape=(
            jax.ShapeDtypeStruct((rows, wide), bf16),
            jax.ShapeDtypeStruct((rows, kv_wide), bf16),
            jax.ShapeDtypeStruct(resp_q.shape, bf16),
            jax.ShapeDtypeStruct(resp_kv.shape, bf16),
        ),
        in_specs=[scalars, scalars, vector] + [any_space] * 6,
        out_specs=(any_space, vector, any_space, any_space),
        scratch_shapes=[
            pltpu.VMEM((rows, wide), bf16),
            pltpu.VMEM((rows, wide), bf16),
            pltpu.VMEM((length, kv_wide), bf16),
            pltpu.VMEM((count, tokens, width), bf16),
            pltpu.VMEM((count, tokens, width), bf16),
            pltpu.VMEM((count, tokens, HEAD_DIM), bf16),
            pltpu.VMEM((count, tokens, HEAD_DIM), bf16),
            pltpu.VMEM((ring, 8, 128), i32),
            pltpu.VMEM((ring, 128), i32),
            pltpu.SMEM((ring, 128), i32),
            pltpu.VMEM((ring, size, HEAD_DIM), bf16),
            pltpu.VMEM((count, ring, size, HEAD_DIM), bf16),
            pltpu.VMEM((count, 2 * length, HEAD_DIM), bf16),
            pltpu.VMEM((length, 2 * rows), f32),
            pltpu.VMEM((length, kv_wide), f32),
            pltpu.VMEM((3, rows, kv_wide), bf16),
            pltpu.VMEM((3, rows, kv_wide), bf16),
            pltpu.VMEM((rows, wide), bf16),
            pltpu.VMEM((count, 2 * length, HEAD_DIM), bf16),
            pltpu.VMEM((count, ring, size, HEAD_DIM), bf16),
            pltpu.VMEM((size // 16, ring * 16, HEAD_DIM), f32),
            pltpu.VMEM((ring, size, HEAD_DIM), bf16),
            pltpu.VMEM((rows, kv_wide), bf16),
            pltpu.VMEM((count, tokens, width), bf16),
            pltpu.VMEM((count, tokens, HEAD_DIM), bf16),
            pltpu.VMEM((count, tokens, HEAD_DIM), bf16),
            dma((8,)),
            dma((3,)),
            dma((3,)),
            dma((2,)),
            dma((CTX,)),
            dma((count,)),
            dma((count,)),
            dma((3,)),
            dma((3,)),
            dma((count,)),
            dma((count,)),
            dma((7, count)),
            dma((7, 2)),
            dma((3,)),
        ],
        compiler_params=pltpu.CompilerParams(
            collective_id=0, has_side_effects=True, vmem_limit_bytes=56 * 1024 * 1024
        ),
        name="attention_gradients",
    )(
        resp_prompt,
        rewards,
        tree_end,
        prompt_q[0],
        prompt_kv[0],
        prompt_cot[0],
        resp_q,
        resp_kv,
        resp_cot,
    )
    return (dpq[None], dpkv[None], drq, drkv)


def solution(mesh):
    in_specs = (
        P("resp", "ctx", None),
        P("resp", "ctx", None),
        P("resp", "ctx", None),
        P("resp", None, None),
        P("resp", None, None),
        P("resp", None, None),
        P("resp", None),
        P("resp", None),
        P("resp"),
    )
    out_specs = (
        P("resp", "ctx", None),
        P("resp", "ctx", None),
        P("resp", None, None),
        P("resp", None, None),
    )
    return jax.shard_map(body, mesh=mesh, in_specs=in_specs, out_specs=out_specs, check_vma=False)
```

time: 656 us -> 125 us (0.19); the launches traced: 648 us -> 124 us
  waiting for transfers between devices: 338 us -> 0 us
  Pallas kernels: 0 us -> 117 us
  blocking collectives: 97.4 us -> 0 us
  matrix products: 94.2 us -> 0 us
  local copies, waits for them, and re-layouts: 78.7 us -> 7.11 us
  other arithmetic: 23.6 us -> 0 us
  between operations: 14.9 us -> 0.66 us
    reduce_scatter x2 -> x0, waiting for transfers between devices: 222 us -> none  [the longest x1 222 us: body(): lax.psum_scatter(per_prompt.astype(jnp.bfloat16), 'resp', scatter_dimensi...]
    pallas_call x0 -> x1, Pallas kernels: none -> 117 us  [body(): pl.pallas_call(functools.partial(kernel, ring), out_shape=(jax.ShapeDtype...]
    dot_general x19 -> x0, matrix products: 94.2 us -> none  [the longest x3 21.4 us: attend(): jnp.einsum('rlkgd,rmkd->rkglm', cotangent, entry[1], preferred_element_ty...]
    psum x2 -> x0, waiting for transfers between devices: 88 us -> none  [the longest x1 66.4 us: body(): lax.psum(grad_query.reshape(responses_here, resp_length, HEADS * HEAD_DIM...]
    psum x1 -> x0, blocking collectives: 84.8 us -> none  [body(): lax.psum((jnp.sum(onehot, axis=0), jnp.sum(onehot * reward_values[:, None...]
    convert_element_type x6 -> x0, local copies, waits for them, and re-layouts: 34.5 us -> none  [the longest x1 21.5 us: body(): per_prompt.astype(jnp.bfloat16)]
    all_gather x2 -> x0, waiting for transfers between devices: 26.4 us -> none  [the longest x1 26.4 us: body(): tiles = lax.all_gather(prompt_kv, 'resp', axis=0, tiled=True)]
    reshape x11 -> x0, local copies, waits for them, and re-layouts: 14.9 us -> none  [the longest x2 5.54 us: body(): key_grads[0][1].reshape(responses_here, prompt_rows, kv_width)]
  transfers between devices with their start and end apart: 6 -> 0, of which waited for: 4 -> 0; matrix products, arithmetic and copies ran while one was open for 25% -> 0% of each run, Pallas kernels for 0% -> 0%
where the time goes in v1:
time: 125 us; the launch traced here: 124 us
  Pallas kernels  117 us (94%)
  local copies, waits for them, and re-layouts  7.11 us (6%)
    pallas_call x1, Pallas kernels, body(): pl.pallas_call(functools.partial(kernel, ring), out_shape=(jax.ShapeDtype...  117 us
    unnamed x11, local copies, waits for them, and re-layouts  7.11 us

profile of v1, /device:TPU:1, one launch (start us, length us, event | category | flops | bytes accessed | tf_op | source)
XLA Modules:
  0.0 124.5 jit_solution(10292238137827542064)
XLA Ops:
  0.6 1.3 %copy.13.routes_in = s32[4,1]{1,0:T(4,128)} copy(s32[4,1]{0,1:T(1,128)} %param.15) | data formatting | bytes 32 | tf_op args[6]
  1.9 116.7 %attention_gradients.1 = (bf16[192,4096]{1,0:T(8,128)(2,1)}, bf16[192,1024]{1,0:T(8,128)(2,1)}, bf16[4,64,4096]{2,1,0:T(8,128)(2,1)}, bf16[4,64,1024]{2,1,0:T(8,128)(2,1)}) custom-call(s32[4,1]{1,0:T(4,128)} %copy.13.routes_in, s32[4]{0:T(128)} %rewards_in.1, s32[4,64]{1,0:T(4,128)} %tree_in.1, bf16[192,4096]{1,0:T(8,128)(2,1)} %bitcast.6, ...), custom_call_target="tpu_custom_call" | custom-call | tf_op jit(solution)/shard_map/attention_gradients/pallas_call | solution.py:634
  118.6 0.0 copy-start.2
  118.6 0.0 copy-start
  118.7 2.9 %copy.18 = bf16[1,192,4096]{2,1,0:T(8,128)(2,1)} copy(bf16[1,192,4096]{2,1,0:T(8,128)(2,1)} %bitcast.5) | data formatting | bytes 3145728
  121.5 0.0 copy-done.2
  121.5 0.7 copy.19
  122.3 0.0 copy-done
  122.3 0.0 copy-start.1
  122.3 1.3 %copy.20 = bf16[4,64,4096]{2,1,0:T(8,128)(2,1)} copy(bf16[4,64,4096]{2,1,0:T(8,128)(2,1)S(1)} %copy-done) | data formatting | bytes 4194304
  123.6 0.1 copy-done.1
  123.7 0.8 copy.21
Async XLA Ops:
  118.6 2.9 %copy-start.2 = (bf16[192,1024]{1,0:T(8,128)(2,1)S(1)}, bf16[192,1024]{1,0:T(8,128)(2,1)}, u32[]{:S(2)}) copy-start(bf16[192,1024]{1,0:T(8,128)(2,1)} %get-tuple-element.9) | copy-start | bytes 1179652
  118.6 3.6 %copy-start = (bf16[4,64,4096]{2,1,0:T(8,128)(2,1)S(1)}, bf16[4,64,4096]{2,1,0:T(8,128)(2,1)}, u32[]{:S(2)}) copy-start(bf16[4,64,4096]{2,1,0:T(8,128)(2,1)} %get-tuple-element.18) | copy-start | bytes 6291460
  122.3 1.4 %copy-start.1 = (bf16[4,64,1024]{2,1,0:T(8,128)(2,1)S(1)}, bf16[4,64,1024]{2,1,0:T(8,128)(2,1)}, u32[]{:S(2)}) copy-start(bf16[4,64,1024]{2,1,0:T(8,128)(2,1)} %get-tuple-element.19) | copy-start | bytes 1572868

commit v2 on v1

v2 whole, which is shorter than its diff:
```python
import functools
import math

import jax
import jax.numpy as jnp
from jax import lax
from jax.experimental import pallas as pl
from jax.experimental.pallas import tpu as pltpu
from jax.sharding import PartitionSpec as P

MESH = pl.DeviceIdType.MESH
KV_HEADS = 4
HEAD_DIM = 128
CTX = 4
ROUTE_ROW = 4
REWARD_ROW = 5
PARTS = 2


def dot_nt(a, b):
    return lax.dot_general(a, b, (((1,), (1,)), ((), ())), preferred_element_type=jnp.float32)


def dot_tn(a, b):
    return lax.dot_general(a, b, (((0,), (0,)), ((), ())), preferred_element_type=jnp.float32)


def dot_nn(a, b):
    return lax.dot_general(a, b, (((1,), (0,)), ((), ())), preferred_element_type=jnp.float32)


def aligned(start, size):
    return pl.ds(pl.multiple_of(start, 16), size)


def columns(start, size):
    return pl.ds(pl.multiple_of(start, 128), size)


def attention_grads(queries, cotangent, pieces, scale):
    to_power = scale * math.log2(math.e)
    scores = []
    for keys, values, adjust in pieces:
        part = dot_nt(keys, queries) * to_power
        scores.append(part if adjust is None else adjust(part))
    highest = functools.reduce(
        jnp.maximum, [jnp.max(part, axis=0, keepdims=True) for part in scores]
    )
    powers = [jnp.exp2(part - highest) for part in scores]
    total = functools.reduce(jnp.add, [jnp.sum(part, axis=0, keepdims=True) for part in powers])
    inverse = 1.0 / total
    grad_probs = [dot_nt(values, cotangent) for keys, values, adjust in pieces]
    delta = inverse * functools.reduce(
        jnp.add,
        [jnp.sum(a * b, axis=0, keepdims=True) for a, b in zip(powers, grad_probs)],
    )
    grad_query = None
    grads = []
    for (keys, values, adjust), power, grad_prob in zip(pieces, powers, grad_probs):
        weight = power * inverse
        narrow = weight.astype(jnp.bfloat16)
        grad_score = (weight * (grad_prob - delta)).astype(jnp.bfloat16)
        grad_values = dot_nn(narrow, cotangent)
        grad_keys = dot_nn(grad_score, queries)
        term = dot_tn(keys, grad_score)
        grad_query = term if grad_query is None else grad_query + term
        grads.append((grad_keys, grad_values))
    return grad_query, grads


def cut(ring):
    halves = 2 if ring >= 16 else 1
    return halves, ring // halves


def kernel(
    ring,
    routes_in,
    rewards_in,
    tree_in,
    pq,
    pkv,
    pcot,
    rq,
    rkv,
    rcot,
    dpq,
    dpkv,
    drq,
    drkv,
    pq_v,
    pcot_v,
    tiles,
    rq_v,
    rcot_v,
    tree_k,
    tree_v,
    notes,
    picks_v,
    picks,
    pieces_in,
    picked,
    chosen,
    bias,
    self_acc,
    self_out,
    self_in,
    grads,
    shares,
    share_acc,
    totals,
    returned,
    sem_load,
    sem_note,
    sem_piece,
    sem_tile_send,
    sem_tile_recv,
    sem_pick_send,
    sem_pick_recv,
    sem_self_send,
    sem_self_recv,
    sem_share_send,
    sem_share_recv,
    sem_query,
    sem_tree,
    sem_total,
):
    scale = 1.0 / math.sqrt(HEAD_DIM)
    c = lax.axis_index("ctx")
    me = lax.axis_index("resp")
    rows = pq.shape[0]
    length = CTX * rows
    count, tokens = rq.shape[0], rq.shape[1]
    group = pq.shape[1] // (KV_HEADS * HEAD_DIM)
    width = group * HEAD_DIM
    half = KV_HEADS * HEAD_DIM
    halves, plane = cut(ring)
    size = 2 * length // plane
    blocks = rows // size
    my_half = me // plane
    my_place = lax.rem(me, plane)
    source = lax.rem(my_place, plane // 2) // blocks
    own_block = lax.rem(my_place, blocks)
    own_kind = my_place // (plane // 2)
    beside = c + 1 - 2 * lax.rem(c, 2)
    across = lax.rem(c + 2, CTX)
    x_size = 4
    y_size = plane // x_size

    def moved(step):
        x = lax.rem(lax.rem(me, x_size) + lax.rem(step, x_size), x_size)
        y = lax.rem(lax.rem(me // x_size, y_size) + lax.rem(step // x_size, y_size), y_size)
        z = lax.rem(my_half + step // plane, halves)
        return z * plane + y * x_size + x

    def remote(src, dst, send, recv, where):
        return pltpu.make_async_remote_copy(
            src_ref=src,
            dst_ref=dst,
            send_sem=send,
            recv_sem=recv,
            device_id=where,
            device_id_type=MESH,
        )

    def settle(ref, sem):
        pltpu.make_async_copy(ref, ref, sem).wait()

    own_tile = pltpu.make_async_copy(pkv, tiles.at[aligned(c * rows, rows)], sem_load.at[0])
    own_tree_k = pltpu.make_async_copy(
        rkv.at[:, :, columns(c * HEAD_DIM, HEAD_DIM)], tree_k, sem_load.at[1]
    )
    own_tree_v = pltpu.make_async_copy(
        rkv.at[:, :, columns(half + c * HEAD_DIM, HEAD_DIM)], tree_v, sem_load.at[2]
    )

    barrier = pltpu.get_barrier_semaphore()

    def greet(step, carry):
        there = (lax.rem(c + step // ring, CTX), lax.rem(me + lax.rem(step, ring), ring))
        pl.semaphore_signal(barrier, inc=1, device_id=there, device_id_type=MESH)
        return carry

    lax.fori_loop(1, CTX * ring, greet, 0)

    own_tile.start()
    own_tree_k.start()
    own_tree_v.start()

    def load_prompt_head(head, carry):
        source_columns = columns(head * HEAD_DIM, HEAD_DIM)
        place = aligned(head * rows, rows)
        pltpu.make_async_copy(pq.at[:, source_columns], pq_v.at[place], sem_load.at[3]).start()
        pltpu.make_async_copy(pcot.at[:, source_columns], pcot_v.at[place], sem_load.at[4]).start()
        return carry

    def load_response_head(head, carry):
        source_columns = columns(c * width + head * HEAD_DIM, HEAD_DIM)
        place = aligned(head * tokens, tokens)
        pltpu.make_async_copy(
            rq.at[:, :, source_columns], rq_v.at[:, place], sem_load.at[5]
        ).start()
        pltpu.make_async_copy(
            rcot.at[:, :, source_columns], rcot_v.at[:, place], sem_load.at[6]
        ).start()
        return carry

    lax.fori_loop(0, KV_HEADS * group, load_prompt_head, 0)
    lax.fori_loop(0, group, load_response_head, 0)

    row = lax.broadcasted_iota(jnp.int32, (8, 128), 0)
    lane = lax.broadcasted_iota(jnp.int32, (8, 128), 1)
    note = jnp.zeros((8, 128), jnp.int32)
    inside = lane // 16 == lax.rem(me, 8)
    for r in range(count):
        route = routes_in[r]
        note = jnp.where((row == r) & inside, route * 16 + lane % 16, note)
        note = jnp.where((row == ROUTE_ROW) & (lane == r), route, note)
        note = jnp.where((row == REWARD_ROW) & (lane == r), rewards_in[r], note)
    notes[me] = note

    pl.semaphore_wait(barrier, CTX * ring - 1)

    def send_note(step, carry):
        there = moved(step)
        remote(notes.at[me], notes.at[me], sem_note.at[0], sem_note.at[1], (c, there)).start()
        return carry

    lax.fori_loop(1, ring, send_note, 0)

    def send_piece(step, carry):
        head = lax.rem(c + step, KV_HEADS)
        part = lax.rem(step // KV_HEADS + my_place, 2 * blocks)
        kind = part // blocks
        block = lax.rem(part, blocks)
        there_half = lax.rem(my_half + step // (KV_HEADS * 2 * blocks), halves)
        there = there_half * plane + kind * (plane // 2) + c * blocks + block
        piece = pkv.at[
            aligned(block * size, size), columns(kind * half + head * HEAD_DIM, HEAD_DIM)
        ]
        here = (head == c) & (there == me)

        @pl.when(here)
        def _():
            pltpu.make_async_copy(piece, pieces_in.at[me], sem_piece.at[2]).start()

        @pl.when(jnp.logical_not(here))
        def _():
            remote(
                piece, pieces_in.at[me], sem_piece.at[0], sem_piece.at[1], (head, there)
            ).start()

        return carry

    piece_count = halves * KV_HEADS * 2 * blocks
    lax.fori_loop(0, piece_count, send_piece, 0)

    def tile(index):
        return tiles.at[pl.ds(index * rows, rows)]

    def send_tile(src, index, slot, where):
        return remote(src, tile(index), sem_tile_send.at[slot], sem_tile_recv.at[index], (where, me))

    @pl.when(c == 0)
    def _():
        send_tile(pkv, 0, 0, 2).start()
        send_tile(pkv, 0, 1, 1).start()

    @pl.when(c == 1)
    def _():
        send_tile(pkv, 1, 0, 3).start()

    @pl.when(c == 2)
    def _():
        send_tile(pkv, 2, 0, 3).start()

    for index in range(1, CTX):

        @pl.when(c < index)
        def _():
            tiles[index * rows : (index + 1) * rows, :] = jnp.zeros((rows, 2 * half), jnp.bfloat16)

    stack = min(4, group)
    position = lax.broadcasted_iota(jnp.int32, (length, rows), 0)
    query = lax.broadcasted_iota(jnp.int32, (length, rows), 1) + c * rows
    allowed_here = jnp.where(position <= query, 0.0, -jnp.inf)
    for index in range(stack):
        bias[:, index * rows : (index + 1) * rows] = allowed_here
    self_acc[...] = jnp.zeros_like(self_acc)
    share_acc[...] = jnp.zeros_like(share_acc)

    settle(notes.at[pl.ds(0, ring - 1)], sem_note.at[1])
    every = notes[...]
    note_row = lax.broadcasted_iota(jnp.int32, every.shape, 1)
    routes = jnp.sum(jnp.where(note_row == ROUTE_ROW, every, 0), axis=1)
    rewards = jnp.sum(jnp.where(note_row == REWARD_ROW, every, 0), axis=1).astype(jnp.float32)
    picks_v[...] = routes
    to_scalars = pltpu.make_async_copy(picks_v, picks, sem_note.at[2])
    to_scalars.start()
    to_scalars.wait()

    @pl.when(c == source)
    def _():
        settle(pieces_in.at[me], sem_piece.at[2])
        settle(pieces_in.at[pl.ds(0, ring - 1)], sem_piece.at[1])

    @pl.when(c != source)
    def _():
        settle(pieces_in, sem_piece.at[1])

    def send_pick(step, carry):
        r = step // (plane - 1)
        there = moved(lax.rem(step, plane - 1) + 1)
        there_place = lax.rem(there, plane)
        picked[r, there_place] = pieces_in[picks[there, r]]
        remote(
            picked.at[r, there_place],
            chosen.at[r, aligned(my_place * size, size)],
            sem_pick_send.at[r],
            sem_pick_recv.at[r],
            (c, there),
        ).start()
        return carry

    lax.fori_loop(0, count * (plane - 1), send_pick, 0)
    for r in range(count):
        chosen[r, aligned(my_place * size, size), :] = pieces_in[picks[me, r]]

    @pl.when(c == 2)
    def _():
        settle(tile(0), sem_tile_recv.at[0])
        send_tile(tile(0), 0, 1, 3).start()
        settle(tile(1), sem_tile_recv.at[1])

    @pl.when(c == 3)
    def _():
        settle(tile(1), sem_tile_recv.at[1])
        send_tile(tile(1), 1, 0, 2).start()
        settle(tile(0), sem_tile_recv.at[0])
        settle(tile(2), sem_tile_recv.at[2])

    @pl.when(c == 1)
    def _():
        settle(tile(0), sem_tile_recv.at[0])

    own_tile.wait()
    own_tree_k.wait()
    own_tree_v.wait()
    settle(pq_v, sem_load.at[3])
    settle(pcot_v, sem_load.at[4])
    settle(rq_v, sem_load.at[5])
    settle(rcot_v, sem_load.at[6])

    parts = group // stack
    together = stack * rows

    def prompt_step(step, carry):
        head = step // parts
        key_columns = columns(head * HEAD_DIM, HEAD_DIM)
        value_columns = columns(half + head * HEAD_DIM, HEAD_DIM)
        place = aligned(step * together, together)
        grad_query, ((grad_keys, grad_values),) = attention_grads(
            pq_v[place, :],
            pcot_v[place, :],
            [(tiles[:, key_columns], tiles[:, value_columns], lambda part: part + bias[...])],
            scale,
        )
        self_acc[:, key_columns] += grad_keys * scale
        self_acc[:, value_columns] += grad_values
        turned = jnp.transpose((grad_query * scale).astype(jnp.bfloat16))
        for index in range(stack):
            dpq[:, columns((step * stack + index) * HEAD_DIM, HEAD_DIM)] = turned[
                index * rows : (index + 1) * rows
            ]
        return carry

    part_width = half // PARTS

    def self_tile(index, part):
        here = slice(index * rows, (index + 1) * rows)
        keys = slice(part * part_width, (part + 1) * part_width)
        values = slice(half + part * part_width, half + (part + 1) * part_width)
        return jnp.concatenate([self_acc[here, keys], self_acc[here, values]], axis=1)

    def send_self(values, part, slot, there, there_slot):
        self_out[part, slot] = values.astype(jnp.bfloat16)
        remote(
            self_out.at[part, slot],
            self_in.at[part, there_slot],
            sem_self_send.at[part, slot],
            sem_self_recv.at[part, there_slot],
            (there, me),
        ).start()

    def prompt_part(part):
        steps = KV_HEADS * parts // PARTS
        lax.fori_loop(part * steps, (part + 1) * steps, prompt_step, 0)

        @pl.when(c == 1)
        def _():
            send_self(self_tile(0, part), part, 0, 0, 0)

        @pl.when(c == 2)
        def _():
            send_self(self_tile(1, part), part, 0, 3, 0)

        @pl.when(c == 3)
        def _():
            send_self(self_tile(0, part), part, 0, 2, 0)
            send_self(self_tile(2, part), part, 1, 2, 1)

    def cross_self(part):
        for core, index in ((2, 0), (3, 1)):

            @pl.when(c == core)
            def _():
                settle(self_in.at[part, 0], sem_self_recv.at[part, 0])
                theirs = self_in[part, 0].astype(jnp.float32)
                send_self(self_tile(index, part) + theirs, part, 2, index, 2)

    prompt_part(0)

    note_lane = lax.broadcasted_iota(jnp.int32, routes.shape, 1)
    for r in range(count):
        same = ((routes == routes_in[r]) & (note_lane < count)).astype(jnp.float32)

        def summed(values):
            return jnp.sum(jnp.sum(values, axis=1, keepdims=True), axis=0, keepdims=True)

        number = summed(same)
        reward_sum = summed(same * rewards)
        reward_square = summed(same * rewards * rewards)
        variance = reward_square * number - reward_sum * reward_sum
        spread = jnp.sqrt(jnp.maximum(variance, number * number)) / number
        own_reward = jnp.full((1, 1), rewards_in[r], jnp.int32).astype(jnp.float32)
        advantage = (own_reward - reward_sum / number) / spread
        rcot_v[r] = (advantage * rcot_v[r].astype(jnp.float32)).astype(jnp.bfloat16)

    key_place = lax.broadcasted_iota(jnp.int32, (tokens, group * tokens), 0)
    query_place = lax.broadcasted_iota(jnp.int32, (tokens, group * tokens), 1) % tokens
    square_row = lax.broadcasted_iota(jnp.int32, (tokens, tokens), 0)
    square_column = lax.broadcasted_iota(jnp.int32, (tokens, tokens), 1)

    def query_rows(r, owner):
        return drq.at[r, :, columns(owner * width, width)]

    def response_step(r, carry):
        settle(chosen.at[r, pl.ds(0, (plane - 1) * size)], sem_pick_recv.at[r])
        ends = tree_in[pl.ds(r, 1), :]
        ends = jnp.sum(
            jnp.where(square_row == square_column, ends, 0), axis=1, keepdims=True
        )
        allowed = (key_place <= query_place) & (query_place < ends)
        grad_query, (prompt_terms, tree_terms) = attention_grads(
            rq_v[r],
            rcot_v[r],
            [
                (chosen[r, :length, :], chosen[r, length:, :], None),
                (tree_k[r], tree_v[r], lambda part: jnp.where(allowed, part, -jnp.inf)),
            ],
            scale,
        )
        grads[r, :length, :] = (prompt_terms[0] * scale).astype(jnp.bfloat16)
        grads[r, length:, :] = prompt_terms[1].astype(jnp.bfloat16)
        drkv[r, :, columns(c * HEAD_DIM, HEAD_DIM)] = (tree_terms[0] * scale).astype(jnp.bfloat16)
        drkv[r, :, columns(half + c * HEAD_DIM, HEAD_DIM)] = tree_terms[1].astype(jnp.bfloat16)
        turned = jnp.transpose((grad_query * scale).astype(jnp.bfloat16))
        drq[r, :, columns(c * width, width)] = jnp.concatenate(
            [turned[g * tokens : (g + 1) * tokens] for g in range(group)], axis=1
        )

        def send_share(step, inner):
            there = moved(step)
            remote(
                grads.at[r, aligned(lax.rem(there, plane) * size, size)],
                shares.at[r, my_place],
                sem_share_send.at[r],
                sem_share_recv.at[r],
                (c, there),
            ).start()
            return inner

        mine = query_rows(r, c)
        remote(mine, mine, sem_query.at[0, r], sem_query.at[1, r], (across, me)).start()
        lax.fori_loop(1, plane, send_share, 0)
        remote(mine, mine, sem_query.at[2, r], sem_query.at[3, r], (beside, me)).start()
        shares[r, my_place] = grads[r, aligned(my_place * size, size), :]
        return carry

    lax.fori_loop(0, count, response_step, 0)

    def tree_part(kind, owner):
        return drkv.at[:, :, columns(kind * half + owner * HEAD_DIM, HEAD_DIM)]

    for kind in range(2):
        mine = tree_part(kind, c)
        remote(mine, mine, sem_tree.at[0, kind], sem_tree.at[1, kind], (across, me)).start()
        remote(mine, mine, sem_tree.at[2, kind], sem_tree.at[3, kind], (beside, me)).start()

    cross_self(0)
    for part in range(1, PARTS):
        prompt_part(part)

    subs = size // 16
    groups = plane // 8

    def share_step(r, carry):
        target = lax.broadcasted_iota(jnp.int32, (ring * 16, 128), 0)
        place = lax.broadcasted_iota(jnp.int32, (8, 8, 128), 1)
        spread = []
        for index in range(groups):
            near = notes[pl.ds(my_half * plane + index * 8, 8)]
            codes = jnp.sum(jnp.where(place == r, near, 0), axis=0)
            codes = jnp.sum(codes, axis=0, keepdims=True)
            spread.append((target == codes).astype(jnp.float32).astype(jnp.bfloat16))
        spread = jnp.concatenate(spread, axis=1)
        settle(shares.at[r, pl.ds(0, plane - 1)], sem_share_recv.at[r])
        for s in range(subs):
            part = shares[r, :, s * 16 : (s + 1) * 16, :].reshape(plane * 16, HEAD_DIM)
            share_acc[s] += dot_nn(spread, part)
        theirs = query_rows(r, across)
        settle(theirs, sem_query.at[1, r])
        remote(theirs, theirs, sem_query.at[4, r], sem_query.at[5, r], (beside, me)).start()
        return carry

    def share_steps(first, last):
        lax.fori_loop(first, last, share_step, 0)

    for part in range(1, PARTS):
        cross_self(part)
    share_steps(0, count)
    for s in range(subs):
        totals[:, s * 16 : (s + 1) * 16, :] = (
            share_acc[s].reshape(ring, 16, HEAD_DIM).astype(jnp.bfloat16)
        )

    home = returned.at[
        my_half,
        aligned(own_block * size, size),
        columns(own_kind * half + c * HEAD_DIM, HEAD_DIM),
    ]

    @pl.when(c == source)
    def _():
        pltpu.make_async_copy(totals.at[me], home, sem_total.at[2]).start()

    @pl.when(c != source)
    def _():
        remote(totals.at[me], home, sem_total.at[0], sem_total.at[1], (source, me)).start()

    def send_total(step, carry):
        there = moved(step)
        remote(
            totals.at[there], home, sem_total.at[0], sem_total.at[1], (source, there)
        ).start()
        return carry

    lax.fori_loop(1, ring, send_total, 0)

    for kind in range(2):
        theirs = tree_part(kind, across)
        settle(theirs, sem_tree.at[1, kind])
        remote(theirs, theirs, sem_tree.at[4, kind], sem_tree.at[5, kind], (beside, me)).start()

    def add_self(part, slot):
        settle(self_in.at[part, slot], sem_self_recv.at[part, slot])
        return self_in[part, slot].astype(jnp.float32)

    own_rows = pl.ds(pl.multiple_of(c * rows, rows), rows)
    for part in range(PARTS):
        keys = slice(part * part_width, (part + 1) * part_width)
        values = slice(half + part * part_width, half + (part + 1) * part_width)

        def add(more):
            self_acc[own_rows, keys] += more[:, :part_width]
            self_acc[own_rows, values] += more[:, part_width:]

        @pl.when(c == 0)
        def _():
            add(add_self(part, 0) + add_self(part, 2))

        @pl.when(c == 1)
        def _():
            add(add_self(part, 2))

        @pl.when(c == 2)
        def _():
            add(add_self(part, 1))

        @pl.when(c >= 1)
        def _():
            settle(self_out.at[part, 0], sem_self_send.at[part, 0])

        @pl.when(c == 3)
        def _():
            settle(self_out.at[part, 1], sem_self_send.at[part, 1])

        @pl.when(c >= 2)
        def _():
            settle(self_out.at[part, 2], sem_self_send.at[part, 2])

    settle(notes.at[pl.ds(0, ring - 1)], sem_note.at[0])

    @pl.when(c == source)
    def _():
        settle(pieces_in.at[pl.ds(0, piece_count - 1)], sem_piece.at[0])

    @pl.when(c != source)
    def _():
        settle(pieces_in.at[pl.ds(0, piece_count)], sem_piece.at[0])

    @pl.when(c == 0)
    def _():
        send_tile(pkv, 0, 0, 2).wait_send()
        send_tile(pkv, 0, 1, 1).wait_send()

    @pl.when(c == 1)
    def _():
        send_tile(pkv, 1, 0, 3).wait_send()

    @pl.when(c == 2)
    def _():
        send_tile(pkv, 2, 0, 3).wait_send()
        send_tile(tile(0), 0, 1, 3).wait_send()

    @pl.when(c == 3)
    def _():
        send_tile(tile(1), 1, 0, 2).wait_send()

    for r in range(count):
        settle(picked.at[r, pl.ds(0, plane - 1)], sem_pick_send.at[r])
        settle(shares.at[r, pl.ds(0, plane - 1)], sem_share_send.at[r])
        for slot in (0, 2, 3, 4, 5):
            settle(query_rows(r, c), sem_query.at[slot, r])
    for kind in range(2):
        for slot in (0, 2, 3, 4, 5):
            settle(tree_part(kind, c), sem_tree.at[slot, kind])

    @pl.when(c == source)
    def _():
        settle(totals.at[me], sem_total.at[2])
        settle(totals.at[pl.ds(0, ring - 1)], sem_total.at[0])

    @pl.when(c != source)
    def _():
        settle(totals, sem_total.at[0])

    others = halves * KV_HEADS * 2 * blocks

    @pl.when(c == source)
    def _():
        settle(totals.at[pl.ds(0, others - 1)], sem_total.at[1])

    @pl.when(c != source)
    def _():
        settle(totals.at[pl.ds(0, others)], sem_total.at[1])

    dpkv[...] = (
        self_acc[own_rows, :]
        + functools.reduce(jnp.add, [returned[z].astype(jnp.float32) for z in range(halves)])
    ).astype(jnp.bfloat16)


def body(
    prompt_q, prompt_kv, prompt_cot, resp_q, resp_kv, resp_cot, resp_prompt, tree_end, rewards
):
    ring = lax.axis_size("resp")
    rows, wide = prompt_q.shape[1:]
    kv_wide = prompt_kv.shape[2]
    count, tokens = resp_q.shape[:2]
    length = CTX * rows
    group = wide // (KV_HEADS * HEAD_DIM)
    width = group * HEAD_DIM
    halves, plane = cut(ring)
    size = 2 * length // plane
    bf16, f32, i32 = jnp.bfloat16, jnp.float32, jnp.int32
    any_space = pl.BlockSpec(memory_space=pl.ANY)
    scalars = pl.BlockSpec(memory_space=pltpu.SMEM)
    vector = pl.BlockSpec(memory_space=pltpu.VMEM)
    dma = pltpu.SemaphoreType.DMA
    dpq, dpkv, drq, drkv = pl.pallas_call(
        functools.partial(kernel, ring),
        out_shape=(
            pltpu.VMEM((rows, wide), bf16),
            pltpu.VMEM((rows, kv_wide), bf16),
            pltpu.VMEM(resp_q.shape, bf16),
            pltpu.VMEM(resp_kv.shape, bf16),
        ),
        in_specs=[scalars, scalars, vector] + [any_space] * 6,
        out_specs=(vector,) * 4,
        scratch_shapes=[
            pltpu.VMEM((wide // HEAD_DIM * rows, HEAD_DIM), bf16),
            pltpu.VMEM((wide // HEAD_DIM * rows, HEAD_DIM), bf16),
            pltpu.VMEM((length, kv_wide), bf16),
            pltpu.VMEM((count, group * tokens, HEAD_DIM), bf16),
            pltpu.VMEM((count, group * tokens, HEAD_DIM), bf16),
            pltpu.VMEM((count, tokens, HEAD_DIM), bf16),
            pltpu.VMEM((count, tokens, HEAD_DIM), bf16),
            pltpu.VMEM((ring, 8, 128), i32),
            pltpu.VMEM((ring, 128), i32),
            pltpu.SMEM((ring, 128), i32),
            pltpu.VMEM((ring, size, HEAD_DIM), bf16),
            pltpu.VMEM((count, plane, size, HEAD_DIM), bf16),
            pltpu.VMEM((count, 2 * length, HEAD_DIM), bf16),
            pltpu.VMEM((length, min(4, group) * rows), f32),
            pltpu.VMEM((length, kv_wide), f32),
            pltpu.VMEM((PARTS, 3, rows, kv_wide // PARTS), bf16),
            pltpu.VMEM((PARTS, 3, rows, kv_wide // PARTS), bf16),
            pltpu.VMEM((count, 2 * length, HEAD_DIM), bf16),
            pltpu.VMEM((count, plane, size, HEAD_DIM), bf16),
            pltpu.VMEM((size // 16, ring * 16, HEAD_DIM), f32),
            pltpu.VMEM((ring, size, HEAD_DIM), bf16),
            pltpu.VMEM((halves, rows, kv_wide), bf16),
            dma((7,)),
            dma((3,)),
            dma((3,)),
            dma((2,)),
            dma((CTX,)),
            dma((count,)),
            dma((count,)),
            dma((PARTS, 3)),
            dma((PARTS, 3)),
            dma((count,)),
            dma((count,)),
            dma((6, count)),
            dma((6, 2)),
            dma((3,)),
        ],
        compiler_params=pltpu.CompilerParams(
            collective_id=0, has_side_effects=True, vmem_limit_bytes=52 * 1024 * 1024
        ),
        name="attention_gradients",
    )(
        resp_prompt[:, 0],
        rewards,
        tree_end,
        prompt_q[0],
        prompt_kv[0],
        prompt_cot[0],
        resp_q,
        resp_kv,
        resp_cot,
    )
    return (dpq[None], dpkv[None], drq, drkv)


def solution(mesh):
    in_specs = (
        P("resp", "ctx", None),
        P("resp", "ctx", None),
        P("resp", "ctx", None),
        P("resp", None, None),
        P("resp", None, None),
        P("resp", None, None),
        P("resp", None),
        P("resp", None),
        P("resp"),
    )
    out_specs = (
        P("resp", "ctx", None),
        P("resp", "ctx", None),
        P("resp", None, None),
        P("resp", None, None),
    )
    return jax.shard_map(body, mesh=mesh, in_specs=in_specs, out_specs=out_specs, check_vma=False)
```

time: 125 us -> 93.7 us (0.75)
  Pallas kernels: 117 us -> 88.9 us
  local copies, waits for them, and re-layouts: 7.11 us -> 4 us
    pallas_call x1, Pallas kernels: 117 us -> 88.9 us  [body(): pl.pallas_call(functools.partial(kernel, ring), out_shape=(pltpu.VMEM((ro...]
    unnamed x11 -> x4, local copies, waits for them, and re-layouts: 7.11 us -> 4 us
where the time goes in v2:
time: 93.7 us; the launch traced here: 93.6 us
  Pallas kernels  88.9 us (95%)
  local copies, waits for them, and re-layouts  4 us (4%)
    pallas_call x1, Pallas kernels, body(): pl.pallas_call(functools.partial(kernel, ring), out_shape=(pltpu.VMEM((ro...  88.9 us
    unnamed x4, local copies, waits for them, and re-layouts  4 us

profile of v2, /device:TPU:1, one launch (start us, length us, event | category | flops | bytes accessed | tf_op | source)
XLA Modules:
  0.0 93.6 jit_solution(9968574455882946374)
XLA Ops:
  0.6 88.9 %attention_gradients.1 = (bf16[192,4096]{1,0:T(8,128)(2,1)S(1)}, bf16[192,1024]{1,0:T(8,128)(2,1)S(1)}, bf16[4,64,4096]{2,1,0:T(8,128)(2,1)S(1)}, bf16[4,64,1024]{2,1,0:T(8,128)(2,1)S(1)}) custom-call(s32[4]{0:T(128)} %bitcast.11, s32[4]{0:T(128)} %rewards_in.1, s32[4,64]{1,0:T(4,128)} %tree_in.1, bf16[192,4096]{1,0:T(8,128)(2,1)} %bitcast.8, ...), custom_call_target="tpu_custom_call" | custom-call | tf_op jit(solution)/shard_map/attention_gradients/pallas_call | solution.py:681
  89.6 1.1 %copy.17 = bf16[1,192,4096]{2,1,0:T(8,128)(2,1)} copy(bf16[1,192,4096]{2,1,0:T(8,128)(2,1)S(1)} %bitcast.6) | data formatting | bytes 3145728
  90.7 0.7 copy.18
  91.4 0.8 copy.20
  92.2 1.3 %copy.19 = bf16[4,64,4096]{2,1,0:T(8,128)(2,1)} copy(bf16[4,64,4096]{2,1,0:T(8,128)(2,1)S(1)} %get-tuple-element.14) | data formatting | bytes 4194304

commit v3 on v2

--- a/solution.py
+++ b/solution.py
@@ -73,6 +73,26 @@
     return halves, ring // halves
 
 
+def place_of(blocks, kind, ctx, block, head, z):
+    if blocks != 2:
+        return (kind * CTX + ctx) * blocks + block
+    high, low = head // 2, head % 2
+    y_high = lax.rem(ctx % 2 + high, 2)
+    y_low = lax.rem(ctx // 2 + high, 2)
+    x_high = lax.rem(kind + high + low + z, 2)
+    x_low = lax.rem(block + low, 2)
+    return ((y_high * 2 + y_low) * 2 + x_high) * 2 + x_low
+
+
+def held_at(blocks, place, head, z):
+    if blocks != 2:
+        return place // (CTX * blocks), lax.rem(place // blocks, CTX), lax.rem(place, blocks)
+    high, low = head // 2, head % 2
+    ctx = lax.rem(place // 8 + high, 2) + 2 * lax.rem(lax.rem(place // 4, 2) + high, 2)
+    kind = lax.rem(lax.rem(place // 2, 2) + high + low + z, 2)
+    return kind, ctx, lax.rem(lax.rem(place, 2) + low, 2)
+
+
 def kernel(
     ring,
     routes_in,
@@ -91,6 +111,7 @@
     pq_v,
     pcot_v,
     tiles,
+    own_columns,
     rq_v,
     rcot_v,
     tree_k,
@@ -139,9 +160,13 @@
     blocks = rows // size
     my_half = me // plane
     my_place = lax.rem(me, plane)
-    source = lax.rem(my_place, plane // 2) // blocks
-    own_block = lax.rem(my_place, blocks)
-    own_kind = my_place // (plane // 2)
+    own_kind, source, own_block = held_at(blocks, my_place, c, my_half)
+
+    def position(place):
+        kind, ctx, block = held_at(blocks, place, c, my_half)
+        return (kind * CTX + ctx) * blocks + block
+
+    my_position = position(my_place)
     beside = c + 1 - 2 * lax.rem(c, 2)
     across = lax.rem(c + 2, CTX)
     x_size = 4
@@ -205,6 +230,13 @@
         ).start()
         return carry
 
+    def load_columns(index, carry):
+        pltpu.make_async_copy(
+            pkv.at[:, columns(index * HEAD_DIM, HEAD_DIM)], own_columns.at[index], sem_load.at[7]
+        ).start()
+        return carry
+
+    lax.fori_loop(0, 2 * KV_HEADS, load_columns, 0)
     lax.fori_loop(0, KV_HEADS * group, load_prompt_head, 0)
     lax.fori_loop(0, group, load_response_head, 0)
 
@@ -219,14 +251,8 @@
         note = jnp.where((row == REWARD_ROW) & (lane == r), rewards_in[r], note)
     notes[me] = note
 
+    settle(own_columns, sem_load.at[7])
     pl.semaphore_wait(barrier, CTX * ring - 1)
-
-    def send_note(step, carry):
-        there = moved(step)
-        remote(notes.at[me], notes.at[me], sem_note.at[0], sem_note.at[1], (c, there)).start()
-        return carry
-
-    lax.fori_loop(1, ring, send_note, 0)
 
     def send_piece(step, carry):
         head = lax.rem(c + step, KV_HEADS)
@@ -234,10 +260,9 @@
         kind = part // blocks
         block = lax.rem(part, blocks)
         there_half = lax.rem(my_half + step // (KV_HEADS * 2 * blocks), halves)
-        there = there_half * plane + kind * (plane // 2) + c * blocks + block
-        piece = pkv.at[
-            aligned(block * size, size), columns(kind * half + head * HEAD_DIM, HEAD_DIM)
-        ]
+        place = place_of(blocks, kind, c, block, head, there_half)
+        there = there_half * plane + place
+        piece = own_columns.at[kind * KV_HEADS + head, aligned(block * size, size)]
         here = (head == c) & (there == me)
 
         @pl.when(here)
@@ -250,6 +275,11 @@
                 piece, pieces_in.at[me], sem_piece.at[0], sem_piece.at[1], (head, there)
             ).start()
 
+        @pl.when(step > 0)
+        def _():
+            note_there = (c, moved(step))
+            remote(notes.at[me], notes.at[me], sem_note.at[0], sem_note.at[1], note_there).start()
+
         return carry
 
     piece_count = halves * KV_HEADS * 2 * blocks
@@ -281,9 +311,9 @@
             tiles[index * rows : (index + 1) * rows, :] = jnp.zeros((rows, 2 * half), jnp.bfloat16)
 
     stack = min(4, group)
-    position = lax.broadcasted_iota(jnp.int32, (length, rows), 0)
+    key = lax.broadcasted_iota(jnp.int32, (length, rows), 0)
     query = lax.broadcasted_iota(jnp.int32, (length, rows), 1) + c * rows
-    allowed_here = jnp.where(position <= query, 0.0, -jnp.inf)
+    allowed_here = jnp.where(key <= query, 0.0, -jnp.inf)
     for index in range(stack):
         bias[:, index * rows : (index + 1) * rows] = allowed_here
     self_acc[...] = jnp.zeros_like(self_acc)
@@ -315,7 +345,7 @@
         picked[r, there_place] = pieces_in[picks[there, r]]
         remote(
             picked.at[r, there_place],
-            chosen.at[r, aligned(my_place * size, size)],
+            chosen.at[r, aligned(my_position * size, size)],
             sem_pick_send.at[r],
             sem_pick_recv.at[r],
             (c, there),
@@ -324,7 +354,7 @@
 
     lax.fori_loop(0, count * (plane - 1), send_pick, 0)
     for r in range(count):
-        chosen[r, aligned(my_place * size, size), :] = pieces_in[picks[me, r]]
+        chosen[r, aligned(my_position * size, size), :] = pieces_in[picks[me, r]]
 
     @pl.when(c == 2)
     def _():
@@ -472,7 +502,7 @@
         def send_share(step, inner):
             there = moved(step)
             remote(
-                grads.at[r, aligned(lax.rem(there, plane) * size, size)],
+                grads.at[r, aligned(position(lax.rem(there, plane)) * size, size)],
                 shares.at[r, my_place],
                 sem_share_send.at[r],
                 sem_share_recv.at[r],
@@ -484,7 +514,7 @@
         remote(mine, mine, sem_query.at[0, r], sem_query.at[1, r], (across, me)).start()
         lax.fori_loop(1, plane, send_share, 0)
         remote(mine, mine, sem_query.at[2, r], sem_query.at[3, r], (beside, me)).start()
-        shares[r, my_place] = grads[r, aligned(my_place * size, size), :]
+        shares[r, my_place] = grads[r, aligned(my_position * size, size), :]
         return carry
 
     lax.fori_loop(0, count, response_step, 0)
@@ -534,11 +564,7 @@
             share_acc[s].reshape(ring, 16, HEAD_DIM).astype(jnp.bfloat16)
         )
 
-    home = returned.at[
-        my_half,
-        aligned(own_block * size, size),
-        columns(own_kind * half + c * HEAD_DIM, HEAD_DIM),
-    ]
+    home = returned.at[my_half, own_kind * KV_HEADS + c, aligned(own_block * size, size)]
 
     @pl.when(c == source)
     def _():
@@ -655,10 +681,24 @@
     def _():
         settle(totals.at[pl.ds(0, others)], sem_total.at[1])
 
-    dpkv[...] = (
-        self_acc[own_rows, :]
-        + functools.reduce(jnp.add, [returned[z].astype(jnp.float32) for z in range(halves)])
-    ).astype(jnp.bfloat16)
+    for index in range(2 * KV_HEADS):
+        here = slice(index * HEAD_DIM, (index + 1) * HEAD_DIM)
+        total = self_acc[own_rows, here]
+        for z in range(halves):
+            total = total + returned[z, index].astype(jnp.float32)
+        dpkv[:, here] = total.astype(jnp.bfloat16)
+
+
+def store(count, *refs):
+    sources, targets, sems = refs[:count], refs[count : 2 * count], refs[2 * count]
+    copies = [
+        pltpu.make_async_copy(source, target, sems.at[index])
+        for index, (source, target) in enumerate(zip(sources, targets))
+    ]
+    for copy in copies:
+        copy.start()
+    for copy in copies:
+        copy.wait()
 
 
 def body(
@@ -692,6 +732,7 @@
             pltpu.VMEM((wide // HEAD_DIM * rows, HEAD_DIM), bf16),
             pltpu.VMEM((wide // HEAD_DIM * rows, HEAD_DIM), bf16),
             pltpu.VMEM((length, kv_wide), bf16),
+            pltpu.VMEM((kv_wide // HEAD_DIM, rows, HEAD_DIM), bf16),
             pltpu.VMEM((count, group * tokens, HEAD_DIM), bf16),
             pltpu.VMEM((count, group * tokens, HEAD_DIM), bf16),
             pltpu.VMEM((count, tokens, HEAD_DIM), bf16),
@@ -710,8 +751,8 @@
             pltpu.VMEM((count, plane, size, HEAD_DIM), bf16),
             pltpu.VMEM((size // 16, ring * 16, HEAD_DIM), f32),
             pltpu.VMEM((ring, size, HEAD_DIM), bf16),
-            pltpu.VMEM((halves, rows, kv_wide), bf16),
-            dma((7,)),
+            pltpu.VMEM((halves, kv_wide // HEAD_DIM, rows, HEAD_DIM), bf16),
+            dma((8,)),
             dma((3,)),
             dma((3,)),
             dma((2,)),
@@ -741,6 +782,16 @@
         resp_kv,
         resp_cot,
     )
+    results = (dpq, dpkv, drq, drkv)
+    dpq, dpkv, drq, drkv = pl.pallas_call(
+        functools.partial(store, len(results)),
+        out_shape=[jax.ShapeDtypeStruct(result.shape, result.dtype) for result in results],
+        in_specs=[vector] * len(results),
+        out_specs=[any_space] * len(results),
+        scratch_shapes=[dma((len(results),))],
+        compiler_params=pltpu.CompilerParams(vmem_limit_bytes=16 * 1024 * 1024),
+        name="store_outputs",
+    )(*results)
     return (dpq[None], dpkv[None], drq, drkv)
 
 

time: 93.7 us -> 85.4 us (0.911)
  Pallas kernels: 88.9 us -> 84.6 us
  local copies, waits for them, and re-layouts: 4 us -> 0 us
    pallas_call x1, Pallas kernels: 88.9 us -> 82.5 us  [body(): pl.pallas_call(functools.partial(kernel, ring), out_shape=(pltpu.VMEM((ro...]
    unnamed x4 -> x0, local copies, waits for them, and re-layouts: 4 us -> none
    pallas_call x0 -> x1, Pallas kernels: none -> 2.17 us  [body(): pl.pallas_call(functools.partial(store, len(results)), out_shape=[jax.Sha...]
where the time goes in v3:
time: 85.4 us; the launch traced here: 85.3 us
  Pallas kernels  84.6 us (99%)
    pallas_call x1, Pallas kernels, body(): pl.pallas_call(functools.partial(kernel, ring), out_shape=(pltpu.VMEM((ro...  82.5 us
    pallas_call x1, Pallas kernels, body(): pl.pallas_call(functools.partial(store, len(results)), out_shape=[jax.Sha...  2.17 us

profile of v3, /device:TPU:1, one launch (start us, length us, event | category | flops | bytes accessed | tf_op | source)
XLA Modules:
  0.0 85.3 jit_solution(5659202761544497112)
XLA Ops:
  0.6 82.5 %attention_gradients.1 = (bf16[192,4096]{1,0:T(8,128)(2,1)S(1)}, bf16[192,1024]{1,0:T(8,128)(2,1)S(1)}, bf16[4,64,4096]{2,1,0:T(8,128)(2,1)S(1)}, bf16[4,64,1024]{2,1,0:T(8,128)(2,1)S(1)}) custom-call(s32[4]{0:T(128)} %bitcast.9, s32[4]{0:T(128)} %rewards_in.1, s32[4,64]{1,0:T(4,128)} %tree_in.1, bf16[192,4096]{1,0:T(8,128)(2,1)} %bitcast.6, ...), custom_call_target="tpu_custom_call" | custom-call | tf_op jit(solution)/shard_map/attention_gradients/pallas_call | solution.py:721
  83.1 2.2 %store_outputs.1 = (bf16[192,4096]{1,0:T(8,128)(2,1)}, bf16[192,1024]{1,0:T(8,128)(2,1)}, bf16[4,64,4096]{2,1,0:T(8,128)(2,1)}, bf16[4,64,1024]{2,1,0:T(8,128)(2,1)}) custom-call(bf16[192,4096]{1,0:T(8,128)(2,1)S(1)} %get-tuple-element.12.refs_0_, bf16[192,1024]{1,0:T(8,128)(2,1)S(1)} %get-tuple-element.13.refs_1_, ...), custom_call_target="tpu_custom_call" | custom-call | tf_op jit(solution)/shard_map/store_outputs/pallas_call | solution.py:786

commit v4 on v3

--- a/solution.py
+++ b/solution.py
@@ -254,12 +254,14 @@
     settle(own_columns, sem_load.at[7])
     pl.semaphore_wait(barrier, CTX * ring - 1)
 
+    piece_count = halves * KV_HEADS * 2 * blocks
+
     def send_piece(step, carry):
-        head = lax.rem(c + step, KV_HEADS)
-        part = lax.rem(step // KV_HEADS + my_place, 2 * blocks)
-        kind = part // blocks
-        block = lax.rem(part, blocks)
-        there_half = lax.rem(my_half + step // (KV_HEADS * 2 * blocks), halves)
+        index = lax.rem(step + me, piece_count)
+        head = lax.rem(index // (2 * blocks), KV_HEADS)
+        kind = lax.rem(index, 2 * blocks) // blocks
+        block = lax.rem(index, blocks)
+        there_half = index // (KV_HEADS * 2 * blocks)
         place = place_of(blocks, kind, c, block, head, there_half)
         there = there_half * plane + place
         piece = own_columns.at[kind * KV_HEADS + head, aligned(block * size, size)]
@@ -282,7 +284,6 @@
 
         return carry
 
-    piece_count = halves * KV_HEADS * 2 * blocks
     lax.fori_loop(0, piece_count, send_piece, 0)
 
     def tile(index):
@@ -310,7 +311,7 @@
         def _():
             tiles[index * rows : (index + 1) * rows, :] = jnp.zeros((rows, 2 * half), jnp.bfloat16)
 
-    stack = min(4, group)
+    stack = min(8, group)
     key = lax.broadcasted_iota(jnp.int32, (length, rows), 0)
     query = lax.broadcasted_iota(jnp.int32, (length, rows), 1) + c * rows
     allowed_here = jnp.where(key <= query, 0.0, -jnp.inf)
@@ -743,7 +744,7 @@
             pltpu.VMEM((ring, size, HEAD_DIM), bf16),
             pltpu.VMEM((count, plane, size, HEAD_DIM), bf16),
             pltpu.VMEM((count, 2 * length, HEAD_DIM), bf16),
-            pltpu.VMEM((length, min(4, group) * rows), f32),
+            pltpu.VMEM((length, min(8, group) * rows), f32),
             pltpu.VMEM((length, kv_wide), f32),
             pltpu.VMEM((PARTS, 3, rows, kv_wide // PARTS), bf16),
             pltpu.VMEM((PARTS, 3, rows, kv_wide // PARTS), bf16),

time: 85.4 us -> 84.1 us (0.985)
  Pallas kernels: 84.6 us -> 83.3 us
    pallas_call x1, Pallas kernels: 82.5 us -> 81.1 us  [body(): pl.pallas_call(functools.partial(kernel, ring), out_shape=(pltpu.VMEM((ro...]
where the time goes in v4:
time: 84.1 us; the launch traced here: 84 us
  Pallas kernels  83.3 us (99%)
    pallas_call x1, Pallas kernels, body(): pl.pallas_call(functools.partial(kernel, ring), out_shape=(pltpu.VMEM((ro...  81.1 us
    pallas_call x1, Pallas kernels, body(): pl.pallas_call(functools.partial(store, len(results)), out_shape=[jax.Sha...  2.17 us

profile of v4, /device:TPU:1, one launch (start us, length us, event | category | flops | bytes accessed | tf_op | source)
XLA Modules:
  0.0 84.0 jit_solution(12339396362954863105)
XLA Ops:
  0.6 81.1 %attention_gradients.1 = (bf16[192,4096]{1,0:T(8,128)(2,1)S(1)}, bf16[192,1024]{1,0:T(8,128)(2,1)S(1)}, bf16[4,64,4096]{2,1,0:T(8,128)(2,1)S(1)}, bf16[4,64,1024]{2,1,0:T(8,128)(2,1)S(1)}) custom-call(s32[4]{0:T(128)} %bitcast.9, s32[4]{0:T(128)} %rewards_in.1, s32[4,64]{1,0:T(4,128)} %tree_in.1, bf16[192,4096]{1,0:T(8,128)(2,1)} %bitcast.6, ...), custom_call_target="tpu_custom_call" | custom-call | tf_op jit(solution)/shard_map/attention_gradients/pallas_call | solution.py:722
  81.8 2.2 %store_outputs.1 = (bf16[192,4096]{1,0:T(8,128)(2,1)}, bf16[192,1024]{1,0:T(8,128)(2,1)}, bf16[4,64,4096]{2,1,0:T(8,128)(2,1)}, bf16[4,64,1024]{2,1,0:T(8,128)(2,1)}) custom-call(bf16[192,4096]{1,0:T(8,128)(2,1)S(1)} %get-tuple-element.12.refs_0_, bf16[192,1024]{1,0:T(8,128)(2,1)S(1)} %get-tuple-element.13.refs_1_, ...), custom_call_target="tpu_custom_call" | custom-call | tf_op jit(solution)/shard_map/store_outputs/pallas_call | solution.py:787

commit v5 on v4

--- a/solution.py
+++ b/solution.py
@@ -341,7 +341,7 @@
 
     def send_pick(step, carry):
         r = step // (plane - 1)
-        there = moved(lax.rem(step, plane - 1) + 1)
+        there = moved(lax.rem(7 * (lax.rem(step, plane - 1) + 1), plane))
         there_place = lax.rem(there, plane)
         picked[r, there_place] = pieces_in[picks[there, r]]
         remote(
@@ -501,7 +501,7 @@
         )
 
         def send_share(step, inner):
-            there = moved(step)
+            there = moved(lax.rem(7 * step, plane))
             remote(
                 grads.at[r, aligned(position(lax.rem(there, plane)) * size, size)],
                 shares.at[r, my_place],
@@ -557,9 +557,10 @@
     def share_steps(first, last):
         lax.fori_loop(first, last, share_step, 0)
 
+    share_steps(0, count // 2)
     for part in range(1, PARTS):
         cross_self(part)
-    share_steps(0, count)
+    share_steps(count // 2, count)
     for s in range(subs):
         totals[:, s * 16 : (s + 1) * 16, :] = (
             share_acc[s].reshape(ring, 16, HEAD_DIM).astype(jnp.bfloat16)

time: 84.1 us -> 83.9 us (level)
  no operation moved by 1% of the time
where the time goes in v5:
time: 83.9 us; the launch traced here: 83.8 us
  Pallas kernels  83.1 us (99%)
    pallas_call x1, Pallas kernels, body(): pl.pallas_call(functools.partial(kernel, ring), out_shape=(pltpu.VMEM((ro...  80.9 us
    pallas_call x1, Pallas kernels, body(): pl.pallas_call(functools.partial(store, len(results)), out_shape=[jax.Sha...  2.17 us

profile of v5, /device:TPU:1, one launch (start us, length us, event | category | flops | bytes accessed | tf_op | source)
XLA Modules:
  0.0 83.8 jit_solution(16366246341328764432)
XLA Ops:
  0.6 80.9 %attention_gradients.1 = (bf16[192,4096]{1,0:T(8,128)(2,1)S(1)}, bf16[192,1024]{1,0:T(8,128)(2,1)S(1)}, bf16[4,64,4096]{2,1,0:T(8,128)(2,1)S(1)}, bf16[4,64,1024]{2,1,0:T(8,128)(2,1)S(1)}) custom-call(s32[4]{0:T(128)} %bitcast.9, s32[4]{0:T(128)} %rewards_in.1, s32[4,64]{1,0:T(4,128)} %tree_in.1, bf16[192,4096]{1,0:T(8,128)(2,1)} %bitcast.6, ...), custom_call_target="tpu_custom_call" | custom-call | tf_op jit(solution)/shard_map/attention_gradients/pallas_call | solution.py:723
  81.6 2.2 %store_outputs.1 = (bf16[192,4096]{1,0:T(8,128)(2,1)}, bf16[192,1024]{1,0:T(8,128)(2,1)}, bf16[4,64,4096]{2,1,0:T(8,128)(2,1)}, bf16[4,64,1024]{2,1,0:T(8,128)(2,1)}) custom-call(bf16[192,4096]{1,0:T(8,128)(2,1)S(1)} %get-tuple-element.12.refs_0_, bf16[192,1024]{1,0:T(8,128)(2,1)S(1)} %get-tuple-element.13.refs_1_, ...), custom_call_target="tpu_custom_call" | custom-call | tf_op jit(solution)/shard_map/store_outputs/pallas_call | solution.py:788
